TPU v7x, 32 devices: a whole 2x2x4 slice. The times are simulated.
32 devices in a mesh: dp: 16 (over z, y, core), mp: 2 (over x).
Axes of the slice: x: 2, y: 2, z: 4, core: 2. Of those that a mesh axis runs over, the one named last changes fastest.
Arguments:
- tokens: bfloat16 [16, 1024, 384], P('dp'), may hold values from -6 to 6
- cotangent: bfloat16 [16, 1024, 384], P('dp'), may hold values from -6 to 6
- task_ids: int32 [16], P('dp'), may hold values from 0 to 12
- att_routes: int32 [16, 1024, 4], P('dp'), may hold values from 0 to 14, all different within a row; in each aligned block of 1024 rows (0 to 1023, 1024 to 2047, ..., all dimensions but the last counted through in order) at most 384 rows name the same one
- mlp_routes: int32 [16, 1024, 4], P('dp'), may hold values from 0 to 14, all different within a row; in each aligned block of 1024 rows (0 to 1023, 1024 to 2047, ..., all dimensions but the last counted through in order) at most 384 rows name the same one
- valid: int32 [16, 1024], P('dp'), may hold values from 0 to 1, as said below
- gain_one: float32 [384], replicated, may hold values from 0.5 to 1.5
- w_query: bfloat16 [15, 384, 384], P(None, 'dp', 'mp'), may hold values from -0.3125 to 0.3125
- w_key: bfloat16 [384, 384], P('dp', 'mp'), may hold values from -0.3125 to 0.3125
- w_value: bfloat16 [384, 384], P('dp', 'mp'), may hold values from -0.3125 to 0.3125
- w_out: bfloat16 [15, 384, 384], P(None, 'mp', 'dp'), may hold values from -4 to 4
- router_att: float32 [13, 384, 15], replicated, may hold values from -0.15 to 0.15
- gain_two: float32 [384], replicated, may hold values from 0.5 to 1.5
- w_up: bfloat16 [15, 384, 1536], P(None, 'dp', 'mp'), may hold values from -0.3125 to 0.3125
- w_down: bfloat16 [15, 1536, 384], P(None, 'mp', 'dp'), may hold values from -0.15625 to 0.15625
- router_mlp: float32 [13, 384, 15], replicated, may hold values from -0.15 to 0.15
Outputs:
- layer_out: bfloat16 [16, 1024, 384], P('dp')
- grad_tokens: float32 [16, 1024, 384], P('dp')
- grad_gain_one: float32 [384], replicated
- grad_query: float32 [15, 384, 384], P(None, 'dp', 'mp')
- grad_key: float32 [384, 384], P('dp', 'mp')
- grad_value: float32 [384, 384], P('dp', 'mp')
- grad_out: float32 [15, 384, 384], P(None, 'mp', 'dp')
- grad_router_att: float32 [13, 384, 15], replicated
- grad_gain_two: float32 [384], replicated
- grad_up: float32 [15, 384, 1536], P(None, 'dp', 'mp')
- grad_down: float32 [15, 1536, 384], P(None, 'mp', 'dp')
- grad_router_mlp: float32 [13, 384, 15], replicated
Inputs may be any that keep to these rules, and one draw needn't show every extreme that they name: `att_routes`: each patch names 4 different experts; within one image no expert is named by more than 384 patches, a bound that some block reaches. `mlp_routes`: each patch names 4 different experts; within one image no expert is named by more than 384 patches, a bound that some block reaches. The share of valid patches differs from image to image.
All inputs are finite; a program needn't handle non-finite values.
Results may differ from a plain program's by a relative error of at most 0.014.
Values may be sent and summed in bfloat16 or wider, within the bound.
No kernel may reach another device: no remote copies, remote signals or barrier semaphores. Data moves between devices by JAX's collectives and lax.ppermute only.
A program may use at most 256 MiB of HBM per device.

v0:
```python
import jax
import jax.numpy as jnp
from jax import lax
from jax.sharding import PartitionSpec as P

HDIM = 64
EXPERTS = 15
TOP = 4
CAP = 384


norm_eps = 1e-06
highest = lax.Precision.HIGHEST
experts_per_block = 3


def layer_norm(values_in, gain):
    centre = jnp.mean(values_in, axis=-1, keepdims=True)
    shifted = values_in - centre
    spread = jnp.mean(shifted * shifted, axis=-1, keepdims=True)
    return shifted * lax.rsqrt(spread + norm_eps) * gain


def softmax_rows(scores):
    row_max = jnp.max(scores, axis=-1, keepdims=True)
    lifted = jnp.exp(scores - row_max)
    return lifted / jnp.sum(lifted, axis=-1, keepdims=True)


def slots(routes):
    flat_ids = routes.reshape(-1)
    matches = (flat_ids[:, None] == jnp.arange(EXPERTS, dtype=jnp.int32)[None, :]).astype(jnp.int32)
    ranks = jnp.sum((jnp.cumsum(matches, axis=0) - 1) * matches, axis=1)
    placed = flat_ids * CAP + ranks
    serial = jnp.arange(routes.shape[0] * TOP, dtype=jnp.int32)
    owners = jnp.zeros((EXPERTS * CAP,), jnp.int32).at[placed].set(serial)
    filled = jnp.zeros((EXPERTS * CAP,), jnp.int32).at[placed].set(1)
    return (placed.reshape(routes.shape[0], TOP), owners, filled)


def gate_weights(normed, router, task_pick, routes):
    chosen_router = jnp.einsum("it,tde->ide", task_pick, router, precision=highest)
    logits = jnp.einsum("ipd,ide->ipe", normed, chosen_router, precision=highest)
    picker = (routes[:, :, :, None] == jnp.arange(router.shape[2], dtype=jnp.int32)).astype(
        jnp.float32
    )
    chosen = jnp.einsum("ipte,ipe->ipt", picker, logits, precision=highest)
    return softmax_rows(chosen)


def dispatch(inputs, owners, filled):
    rows = jax.vmap(lambda source, index: source[index])(inputs, owners // TOP)
    return rows * filled[:, :, None].astype(inputs.dtype)


def pick_rows(outputs, placed):
    return jax.vmap(lambda source, index: source[index])(outputs, placed)


def combine(outputs, placed, gates):
    picked = pick_rows(outputs, placed)
    return (jnp.einsum("iptd,ipt->ipd", picked, gates), picked)


def spread_back(grads, gates, owners, filled):
    patch_ids = owners // TOP
    choice_ids = owners % TOP
    rows = jax.vmap(lambda source, index: source[index])(grads, patch_ids)
    scale = jax.vmap(lambda source, first, second: source[first, second])(
        gates, patch_ids, choice_ids
    )
    return (rows * (scale * filled.astype(jnp.float32))[:, :, None]).astype(jnp.bfloat16)


def block_forward(query_block, key_image, value_image):
    scores = (
        jnp.einsum("rhd,khd->hrk", query_block, key_image, preferred_element_type=jnp.float32)
        * 0.125
    )
    row_max = jnp.max(scores, axis=-1, keepdims=True)
    lifted = jnp.exp(scores - row_max)
    summed = jnp.sum(lifted, axis=-1, keepdims=True)
    weights = (lifted / summed).astype(jnp.bfloat16)
    mixed = jnp.einsum("hrk,khd->rhd", weights, value_image, preferred_element_type=jnp.float32)
    return (mixed.astype(jnp.bfloat16), (row_max + jnp.log(summed))[:, :, 0])


def attend_forward(queries, keys, values):

    def per_image(packed):
        query_image, key_image, value_image = packed
        return lax.map(
            lambda query_block: block_forward(query_block, key_image, value_image), query_image
        )

    return lax.map(per_image, (queries, keys, values))


def block_backward(running, block_items, key_image, value_image):
    key_grad, value_grad = running
    query_block, log_total, mixed_grad = block_items
    scores = (
        jnp.einsum("rhd,khd->hrk", query_block, key_image, preferred_element_type=jnp.float32)
        * 0.125
    )
    probs = jnp.exp(scores - log_total[:, :, None])
    prob_grad = jnp.einsum(
        "rhd,khd->hrk", mixed_grad, value_image, preferred_element_type=jnp.float32
    )
    score_grad = (probs * (prob_grad - jnp.sum(probs * prob_grad, axis=-1, keepdims=True))).astype(
        jnp.bfloat16
    )
    query_grad = (
        jnp.einsum("hrk,khd->rhd", score_grad, key_image, preferred_element_type=jnp.float32)
        * 0.125
    )
    key_grad = (
        key_grad
        + jnp.einsum("hrk,rhd->khd", score_grad, query_block, preferred_element_type=jnp.float32)
        * 0.125
    )
    value_grad = value_grad + jnp.einsum(
        "hrk,rhd->khd", probs.astype(jnp.bfloat16), mixed_grad, preferred_element_type=jnp.float32
    )
    return ((key_grad, value_grad), query_grad)


def attend_backward(queries, keys, values, log_totals, mixed_grads):

    def per_image(packed):
        query_image, key_image, value_image, log_image, grad_image = packed
        initial = (
            jnp.zeros(key_image.shape, jnp.float32),
            jnp.zeros(value_image.shape, jnp.float32),
        )
        (key_grad, value_grad), query_grad = lax.scan(
            lambda running, block_items: block_backward(
                running, block_items, key_image, value_image
            ),
            initial,
            (query_image, log_image, grad_image),
        )
        return (query_grad, key_grad, value_grad)

    return lax.map(per_image, (queries, keys, values, log_totals, mixed_grads))


def body(
    tokens,
    cotangent,
    task_ids,
    att_routes,
    mlp_routes,
    valid,
    gain_one,
    w_query,
    w_key,
    w_value,
    w_out,
    router_att,
    gain_two,
    w_up,
    w_down,
    router_mlp,
):
    images, patches, width = tokens.shape
    heads_here = w_key.shape[1] // HDIM
    local_hd = w_key.shape[1]
    block_count = EXPERTS // experts_per_block
    query_full, key_full, value_full, out_full, up_full, down_full = (
        lax.all_gather(w_query, "dp", axis=1, tiled=True),
        lax.all_gather(w_key, "dp", axis=0, tiled=True),
        lax.all_gather(w_value, "dp", axis=0, tiled=True),
        lax.all_gather(w_out, "dp", axis=2, tiled=True),
        lax.all_gather(w_up, "dp", axis=1, tiled=True),
        lax.all_gather(w_down, "dp", axis=2, tiled=True),
    )
    placed_att, owners_att, filled_att = jax.vmap(slots)(att_routes)
    placed_mlp, owners_mlp, filled_mlp = jax.vmap(slots)(mlp_routes)
    task_pick = (
        task_ids[:, None] == jnp.arange(router_att.shape[0], dtype=jnp.int32)[None, :]
    ).astype(jnp.float32)
    token_f = tokens.astype(jnp.float32)
    normed_one, norm_one_pull = jax.vjp(layer_norm, token_f, gain_one)
    input_one = normed_one.astype(jnp.bfloat16)
    keys = jnp.dot(input_one, key_full, preferred_element_type=jnp.float32).astype(jnp.bfloat16)
    values = jnp.dot(input_one, value_full, preferred_element_type=jnp.float32).astype(jnp.bfloat16)
    gates_att, gate_att_pull = jax.vjp(
        lambda normed, router: gate_weights(normed, router, task_pick, att_routes),
        normed_one,
        router_att,
    )
    rows_att = dispatch(input_one, owners_att, filled_att).reshape(images, EXPERTS, CAP, width)
    queries = jnp.einsum(
        "iecd,edh->iech", rows_att, query_full, preferred_element_type=jnp.float32
    ).astype(jnp.bfloat16)
    query_blocks = queries.reshape(images, block_count, experts_per_block * CAP, heads_here, HDIM)
    key_heads = keys.reshape(images, patches, heads_here, HDIM)
    value_heads = values.reshape(images, patches, heads_here, HDIM)
    mixed, log_totals = attend_forward(query_blocks, key_heads, value_heads)
    mixed_rows = mixed.reshape(images, EXPERTS, CAP, local_hd)
    outs_att = jnp.einsum(
        "iech,ehd->iecd", mixed_rows, out_full, preferred_element_type=jnp.float32
    ).reshape(images, EXPERTS * CAP, width)
    part_att, picked_att = combine(outs_att, placed_att, gates_att)
    middle = token_f + lax.psum(part_att, "mp")
    normed_two, norm_two_pull = jax.vjp(layer_norm, middle, gain_two)
    input_two = normed_two.astype(jnp.bfloat16)
    gates_mlp, gate_mlp_pull = jax.vjp(
        lambda normed, router: gate_weights(normed, router, task_pick, mlp_routes),
        normed_two,
        router_mlp,
    )
    rows_mlp = dispatch(input_two, owners_mlp, filled_mlp).reshape(images, EXPERTS, CAP, width)
    hidden = jnp.einsum("iecd,edf->iecf", rows_mlp, up_full, preferred_element_type=jnp.float32)
    gelu_out, gelu_pull = jax.vjp(jax.nn.gelu, hidden)
    acts = gelu_out.astype(jnp.bfloat16)
    outs_mlp = jnp.einsum(
        "iecf,efd->iecd", acts, down_full, preferred_element_type=jnp.float32
    ).reshape(images, EXPERTS * CAP, width)
    part_mlp, picked_mlp = combine(outs_mlp, placed_mlp, gates_mlp)
    layer_out = (middle + lax.psum(part_mlp.astype(jnp.bfloat16), "mp").astype(jnp.float32)).astype(
        jnp.bfloat16
    )
    masked_grad = cotangent.astype(jnp.float32) * valid.astype(jnp.float32)[:, :, None]
    gate_grad_mlp = lax.psum(jnp.einsum("iptd,ipd->ipt", picked_mlp, masked_grad), "mp")
    out_grad_mlp = spread_back(masked_grad, gates_mlp, owners_mlp, filled_mlp).reshape(
        images, EXPERTS, CAP, width
    )
    grad_down = jnp.einsum("iecf,iecd->efd", acts, out_grad_mlp, preferred_element_type=jnp.float32)
    act_grad = jnp.einsum(
        "iecd,efd->iecf", out_grad_mlp, down_full, preferred_element_type=jnp.float32
    )
    hidden_grad = gelu_pull(act_grad)[0].astype(jnp.bfloat16)
    grad_up = jnp.einsum(
        "iecd,iecf->edf", rows_mlp, hidden_grad, preferred_element_type=jnp.float32
    )
    rows_grad_mlp = jnp.einsum(
        "iecf,edf->iecd", hidden_grad, up_full, preferred_element_type=jnp.float32
    ).reshape(images, EXPERTS * CAP, width)
    part_two = jnp.sum(pick_rows(rows_grad_mlp, placed_mlp), axis=2)
    norm_two_grad = lax.psum(part_two.astype(jnp.bfloat16), "mp").astype(jnp.float32)
    router_two_grad, grad_router_mlp = gate_mlp_pull(gate_grad_mlp)
    middle_ln_grad, grad_gain_two = norm_two_pull(norm_two_grad + router_two_grad)
    middle_grad = masked_grad + middle_ln_grad
    gate_grad_att = lax.psum(jnp.einsum("iptd,ipd->ipt", picked_att, middle_grad), "mp")
    out_grad_att = spread_back(middle_grad, gates_att, owners_att, filled_att).reshape(
        images, EXPERTS, CAP, width
    )
    grad_out = jnp.einsum(
        "iech,iecd->ehd", mixed_rows, out_grad_att, preferred_element_type=jnp.float32
    )
    mixed_grad = jnp.einsum(
        "iecd,ehd->iech", out_grad_att, out_full, preferred_element_type=jnp.float32
    ).astype(jnp.bfloat16)
    mixed_grad_blocks = mixed_grad.reshape(
        images, block_count, experts_per_block * CAP, heads_here, HDIM
    )
    query_grad, key_grad, value_grad = attend_backward(
        query_blocks, key_heads, value_heads, log_totals, mixed_grad_blocks
    )
    query_grad = query_grad.reshape(images, EXPERTS, CAP, local_hd).astype(jnp.bfloat16)
    key_grad = key_grad.reshape(images, patches, local_hd).astype(jnp.bfloat16)
    value_grad = value_grad.reshape(images, patches, local_hd).astype(jnp.bfloat16)
    grad_query = jnp.einsum(
        "iecd,iech->edh", rows_att, query_grad, preferred_element_type=jnp.float32
    )
    grad_key = jnp.einsum("ipd,iph->dh", input_one, key_grad, preferred_element_type=jnp.float32)
    grad_value = jnp.einsum(
        "ipd,iph->dh", input_one, value_grad, preferred_element_type=jnp.float32
    )
    rows_grad_att = jnp.einsum(
        "iech,edh->iecd", query_grad, query_full, preferred_element_type=jnp.float32
    ).reshape(images, EXPERTS * CAP, width)
    part_one = jnp.sum(pick_rows(rows_grad_att, placed_att), axis=2)
    part_one = part_one + jnp.einsum(
        "iph,dh->ipd", key_grad, key_full, preferred_element_type=jnp.float32
    )
    part_one = part_one + jnp.einsum(
        "iph,dh->ipd", value_grad, value_full, preferred_element_type=jnp.float32
    )
    norm_one_grad = lax.psum(part_one.astype(jnp.bfloat16), "mp").astype(jnp.float32)
    router_one_grad, grad_router_att = gate_att_pull(gate_grad_att)
    token_ln_grad, grad_gain_one = norm_one_pull(norm_one_grad + router_one_grad)
    grad_tokens = middle_grad + token_ln_grad
    grad_query, grad_key, grad_value, grad_out, grad_up, grad_down = (
        lax.psum_scatter(grad_query, "dp", scatter_dimension=1, tiled=True),
        lax.psum_scatter(grad_key, "dp", scatter_dimension=0, tiled=True),
        lax.psum_scatter(grad_value, "dp", scatter_dimension=0, tiled=True),
        lax.psum_scatter(grad_out, "dp", scatter_dimension=2, tiled=True),
        lax.psum_scatter(grad_up, "dp", scatter_dimension=1, tiled=True),
        lax.psum_scatter(grad_down, "dp", scatter_dimension=2, tiled=True),
    )
    grad_gain_one, grad_router_att, grad_gain_two, grad_router_mlp = lax.psum(
        (grad_gain_one, grad_router_att, grad_gain_two, grad_router_mlp), "dp"
    )
    return (
        layer_out,
        grad_tokens,
        grad_gain_one,
        grad_query,
        grad_key,
        grad_value,
        grad_out,
        grad_router_att,
        grad_gain_two,
        grad_up,
        grad_down,
        grad_router_mlp,
    )


def solution(mesh):
    return jax.shard_map(
        body,
        mesh=mesh,
        in_specs=(
            P("dp", None, None),
            P("dp", None, None),
            P("dp"),
            P("dp", None, None),
            P("dp", None, None),
            P("dp", None),
            P(),
            P(None, "dp", "mp"),
            P("dp", "mp"),
            P("dp", "mp"),
            P(None, "mp", "dp"),
            P(),
            P(),
            P(None, "dp", "mp"),
            P(None, "mp", "dp"),
            P(),
        ),
        out_specs=(
            P("dp", None, None),
            P("dp", None, None),
            P(),
            P(None, "dp", "mp"),
            P("dp", "mp"),
            P("dp", "mp"),
            P(None, "mp", "dp"),
            P(),
            P(),
            P(None, "dp", "mp"),
            P(None, "mp", "dp"),
            P(),
        ),
        check_vma=False,
    )
```

profile of v0, /device:TPU:0, one launch (start us, length us, event | category | flops | bytes accessed | tf_op | source)
XLA Modules:
  0.0 2084.7 jit_solution(13968676911966483380)
XLA Ops:
  26.4 15.5 scatter_custom_fusion
  44.4 40.9 %gather_fusion = bf16[5760,384]{1,0:T(8,128)(2,1)} fusion(bf16[1,1024,384]{2,1,0:T(8,128)(2,1)S(1)} %copy.245, s32[5760]{0:T(1024)S(1)} %fusion.164), kind=kCustom, calls=%fused_computation | custom fusion | bytes 8893440 | tf_op jit(solution)/shard_map/vmap()/gather | solution.py:52
  91.9 15.5 scatter_custom_fusion.1
  107.5 23.6 %all_gather.19 = bf16[384,192]{1,0:T(8,128)(2,1)S(1)} all-gather(bf16[24,192]{1,0:T(8,128)(2,1)S(1)} %copy-done.96), channel_id=1, replica_groups=mesh['dp'=16,'mp'=2] {'dp'}, dimensions={0}, use_global_device_ids=true | all-gather | bytes 156672 | tf_op jit(solution)/shard_map/all_gather | solution.py:172
  133.0 18.2 all_gather.20
  170.5 55.4 %while.47 = (s32[]{:T(128)}, bf16[5,1152,3,64]{1,3,2,0:T(8,128)(2,1)}, f32[5,3,1152]{2,1,0:T(4,128)}, bf16[5,1152,3,64]{1,3,2,0:T(8,128)(2,1)}, bf16[1024,3,64]{...) while((s32[]{:T(128)}, bf16[5,1152,3,64]{1,3,2,0:T(8,128)(2,1)}, f32[5,3,1152]{2,1,0:T(4,128)}, ...), condition=%wide.region_10.11_spmd, body=%wide.region_7.0_spmd.sunk | while | flops 938037888 | bytes 44255308 | solution.py:92
  241.5 65.8 %gather_fusion.1 = bf16[4096,384]{1,0:T(8,128)(2,1)} fusion(bf16[1,5760,384]{2,1,0:T(8,128)(2,1)} %bitcast.417, s32[4096]{0:T(1024)S(1)} %reshape.1032), kind=kCustom, calls=%fused_computation.1 | custom fusion | bytes 6324224 | tf_op jit(solution)/shard_map/vmap()/gather | solution.py:57
  323.4 15.7 scatter_custom_fusion.3
  339.1 15.7 scatter_custom_fusion.2
  358.9 42.4 %gather_fusion.4 = f32[5760,384]{1,0:T(8,128)} fusion(f32[1,1024,384]{2,1,0:T(8,128)S(1)} %copy.265, s32[5760]{0:T(1024)S(1)} %fusion.165), kind=kCustom, calls=%fused_computation.4 | custom fusion | bytes 17740800 | tf_op jit(solution)/shard_map/vmap()/gather | solution.py:68
  401.3 9.6 copy.266
  418.3 35.2 %gather_fusion.8 = f32[5760]{0:T(1024)S(1)} fusion(f32[1,1024,4]{2,1,0:T(8,128)S(1)} %bitcast.412, s32[5760]{0:T(1024)S(1)} %fusion.167), kind=kCustom, calls=%fused_computation.8 | custom fusion | bytes 115200 | tf_op jit(solution)/shard_map/vmap()/gather | solution.py:69
  461.0 35.2 %gather_fusion.5 = f32[5760]{0:T(1024)S(1)} fusion(f32[1,1024,4]{2,1,0:T(8,128)S(1)} %bitcast.413, s32[5760]{0:T(1024)S(1)} %fusion.166), kind=kCustom, calls=%fused_computation.5 | custom fusion | bytes 115200 | tf_op jit(solution)/shard_map/vmap()/gather | solution.py:69
  498.8 40.8 %gather_fusion.2 = bf16[5760,384]{1,0:T(8,128)(2,1)} fusion(bf16[1,1024,384]{2,1,0:T(8,128)(2,1)S(1)} %copy.259, s32[5760]{0:T(1024)S(1)} %fusion.165), kind=kCustom, calls=%fused_computation.2 | custom fusion | bytes 8893440 | tf_op jit(solution)/shard_map/vmap()/gather | solution.py:52
  546.4 15.7 fusion.55
  562.2 13.6 fusion.52
  575.8 65.8 %gather_fusion.3 = bf16[4096,384]{1,0:T(8,128)(2,1)} fusion(bf16[1,5760,384]{2,1,0:T(8,128)(2,1)} %bitcast.418, s32[4096]{0:T(1024)S(1)} %reshape.1048), kind=kCustom, calls=%fused_computation.3 | custom fusion | bytes 6324224 | tf_op jit(solution)/shard_map/vmap()/gather | solution.py:57
  653.4 17.9 psum.73
  672.4 22.6 %fusion.41 = bf16[1,15,384,768]{3,2,1,0:T(8,128)(2,1)} fusion(f32[15,384,768]{2,1,0:T(8,128)} %fusion.55, bf16[15,768,384]{1,2,0:T(8,128)(2,1)} %all-gather.11.cloned.1.call-done, f32[15,384,384]{1,2,0:T(8,128)} %copy.266, f32[15,384]{1,0:T(8,128)S(1)} %mul.382), kind=kOutput, calls=%fused_computation.63 | convolution fusion | flops 3490283520 | bytes 44259840 | tf_op jit(solution)/shard_map/iecd,efd->iecf/dot_general | solution.py:231
  695.0 14.2 fusion.48
  709.2 64.7 %gather_fusion.6 = f32[4096,384]{1,0:T(8,128)} fusion(f32[1,5760,384]{2,1,0:T(8,128)} %bitcast.415, s32[4096]{0:T(1024)S(1)} %reshape.1048), kind=kCustom, calls=%fused_computation.6 | custom fusion | bytes 12615680 | tf_op jit(solution)/shard_map/vmap()/gather | solution.py:57
  806.4 15.9 all-reduce.10.cloned.1.call-done
  837.5 17.9 psum.75
  855.5 42.4 %gather_fusion.7 = f32[5760,384]{1,0:T(8,128)} fusion(f32[1,1024,384]{2,1,0:T(8,128)S(1)} %copy.269, s32[5760]{0:T(1024)S(1)} %copy-done.5), kind=kCustom, calls=%fused_computation.7 | custom fusion | bytes 17740800 | tf_op jit(solution)/shard_map/vmap()/gather | solution.py:68
  897.9 9.5 copy.270
  920.7 227.7 %while.48 = (s32[]{:T(128)}, f32[1024,3,64]{0,2,1:T(8,128)S(1)}, f32[1024,3,64]{0,2,1:T(8,128)S(1)}, bf16[5,1152,3,64]{1,3,2,0:T(8,128)(2,1)}, bf16[5,1152,3,64]...) while((s32[]{:T(128)}, f32[1024,3,64]{0,2,1:T(8,128)S(1)}, ...), condition=%wide.region_34.35_spmd.clone, body=%wide.region_32.34_spmd.clone.sunk | while | flops 2294436352 | bytes 198154416 | solution.py:136
  920.7 8.1 fusion.283
  936.6 11.6 multiply_convert_fusion.8
  966.3 8.1 fusion.283
  982.1 11.6 multiply_convert_fusion.8
  1011.8 8.1 fusion.283
  1027.6 11.6 multiply_convert_fusion.8
  1057.4 8.1 fusion.283
  1073.2 11.6 multiply_convert_fusion.8
  1102.9 8.1 fusion.283
  1118.7 11.6 multiply_convert_fusion.8
  1166.7 64.6 %gather_fusion.9 = f32[4096,384]{1,0:T(8,128)} fusion(f32[1,5760,384]{2,1,0:T(8,128)} %bitcast.416, s32[4096]{0:T(1024)S(1)} %copy-done.10), kind=kCustom, calls=%fused_computation.9 | custom fusion | bytes 12615680 | tf_op jit(solution)/shard_map/vmap()/gather | solution.py:57
  1264.6 8.6 fusion.76
  1282.1 17.7 fusion.50
  1300.6 15.7 fusion.46
  1325.9 31.7 %all-reduce = (f32[384]{0:T(512)}, f32[384]{0:T(512)}) all-reduce(f32[384]{0:T(512)S(1)} %get-tuple-element.323, f32[384]{0:T(512)S(1)} %copy-done.98), channel_id=1, replica_groups=mesh['dp'=16,'mp'=2] {'dp'}, use_global_device_ids=true, to_apply=%region_44.45 | all-reduce | flops 768 | bytes 6144 | tf_op jit(solution)/shard_map/psum | solution.py:294
  1357.6 43.4 %all-reduce.12.cloned.1.call-done = (f32[13,384,15]{1,2,0:T(8,128)}, f32[13,384,15]{1,2,0:T(8,128)}) async-done(((f32[13,384,15]{1,2,0:T(8,128)}, f32[13,384,15]{1,2,0:T(8,128)}), (f32[13,384,15]{1,2,0:T(8,128)}, f32[13,384,15]{1,2,0:T(8,128)})) %all-reduce.12.cloned.1.call-update) | async-done | bytes 599056 | tf_op jit(solution)/shard_map/psum | solution.py:294
  1400.9 60.5 %reduce-scatter.11.cloned.1.call-done = f32[24,192]{1,0:T(8,128)} async-done(((f32[384,192]{1,0:T(8,128)}), f32[24,192]{1,0:T(8,128)}) %reduce-scatter.11.cloned.1.call-update) | async-done | bytes 18448 | tf_op jit(solution)/shard_map/reduce_scatter | solution.py:289
  1461.4 58.6 %reduce-scatter.9.cloned.1.call-done = f32[24,192]{1,0:T(8,128)} async-done(((f32[384,192]{1,0:T(8,128)}), f32[24,192]{1,0:T(8,128)}) %reduce-scatter.9.cloned.1.call-update) | async-done | bytes 18448 | tf_op jit(solution)/shard_map/reduce_scatter | solution.py:288
  1520.0 86.7 %reduce-scatter.13.cloned.1.call-done = f32[15,192,24]{1,2,0:T(8,128)} async-done(((f32[15,192,384]{1,2,0:T(8,128)}), f32[15,192,24]{1,2,0:T(8,128)}) %reduce-scatter.13.cloned.1.call-update) | async-done | bytes 276496 | tf_op jit(solution)/shard_map/reduce_scatter | solution.py:290
  1606.7 86.1 %reduce-scatter.7.cloned.1.call-done = f32[15,24,192]{2,1,0:T(8,128)} async-done(((f32[15,384,192]{2,1,0:T(8,128)}), f32[15,24,192]{2,1,0:T(8,128)}) %reduce-scatter.7.cloned.1.call-update) | async-done | bytes 276496 | tf_op jit(solution)/shard_map/reduce_scatter | solution.py:287
  1692.8 190.8 %reduce-scatter.17.cloned.1.call-done = f32[15,768,24]{1,2,0:T(8,128)} async-done(((f32[15,768,384]{1,2,0:T(8,128)}), f32[15,768,24]{1,2,0:T(8,128)}) %reduce-scatter.17.cloned.1.call-update) | async-done | bytes 1105936 | tf_op jit(solution)/shard_map/reduce_scatter | solution.py:292
  1883.6 190.7 %reduce-scatter.15.cloned.1.call-done = f32[15,24,768]{2,1,0:T(8,128)} async-done(((f32[15,384,768]{2,1,0:T(8,128)}), f32[15,24,768]{2,1,0:T(8,128)}) %reduce-scatter.15.cloned.1.call-update) | async-done | bytes 1105936 | tf_op jit(solution)/shard_map/reduce_scatter | solution.py:291
  (482 shorter events, 439.8 us)
Async XLA Ops:
  7.2 146.4 %copy-start = (f32[13,384,15]{1,2,0:T(8,128)S(1)}, f32[13,384,15]{1,2,0:T(8,128)}, u32[]{:S(2)}) copy-start(f32[13,384,15]{1,2,0:T(8,128)} %param.31) | copy-start | bytes 898564
  7.2 150.6 %all-gather.5.cloned.1.call-start = ((), (), s32[]{:S(2)}) async-start(), calls=%async_computation.6 | async-start | bytes 3133440 | tf_op jit(solution)/shard_map/all_gather | solution.py:171
  8.0 226.9 %all-gather.7.cloned.1.call-start = ((), (), s32[]{:S(2)}) async-start(), calls=%async_computation.7 | async-start | bytes 3133440 | tf_op jit(solution)/shard_map/all_gather | solution.py:174
  8.7 446.8 %all-reduce.8.cloned.1.call-start = ((), (), s32[]{:S(2)}) async-start(), calls=%async_computation.8 | async-start | bytes 3145728 | tf_op jit(solution)/shard_map/psum | solution.py:206
  17.7 25.3 %copy-start.43 = (bf16[1,1024,384]{2,1,0:T(8,128)(2,1)S(1)}, bf16[1,1024,384]{2,1,0:T(8,128)(2,1)}, u32[]{:S(2)}) copy-start(bf16[1,1024,384]{2,1,0:T(8,128)(2,1)} %param.20) | copy-start | bytes 2359300
  24.0 19.7 copy-start.88
  43.3 110.8 %copy-start.15 = (bf16[1,1024,384]{1,2,0:T(8,128)(2,1)}, bf16[1,1024,384]{1,2,0:T(8,128)(2,1)S(1)}, u32[]{:S(2)}) copy-start(bf16[1,1024,384]{1,2,0:T(8,128)(2,1)S(1)} %copy.239) | copy-start | bytes 2359300
  43.5 110.6 %copy-start.65 = (f32[1024]{0:T(1024)}, f32[1024]{0:T(1024)S(1)}, u32[]{:S(2)}) copy-start(f32[1024]{0:T(1024)S(1)} %broadcast_multiply_fusion.5) | copy-start | bytes 12292
  43.7 41.6 %copy-start.84 = (f32[1024]{0:T(1024)}, f32[1024]{0:T(1024)S(1)}, u32[]{:S(2)}) copy-start(f32[1024]{0:T(1024)S(1)} %fusion.89) | copy-start | bytes 12292
  43.7 110.4 %copy-start.74 = (f32[1024]{0:T(1024)}, f32[1024]{0:T(1024)S(1)}, u32[]{:S(2)}) copy-start(f32[1024]{0:T(1024)S(1)} %fusion.184) | copy-start | bytes 12292
  44.0 107.2 %copy-start.20 = (bf16[1,1024,384]{1,2,0:T(8,128)(2,1)}, bf16[1,1024,384]{1,2,0:T(8,128)(2,1)S(1)}, u32[]{:S(2)}) copy-start(bf16[1,1024,384]{1,2,0:T(8,128)(2,1)S(1)} %fusion.83) | copy-start | bytes 2359300
  85.3 22.2 %copy-start.96 = (bf16[24,192]{1,0:T(8,128)(2,1)S(1)}, bf16[24,192]{1,0:T(8,128)(2,1)}, u32[]{:S(2)}) copy-start(bf16[24,192]{1,0:T(8,128)(2,1)} %param.28) | copy-start | bytes 27652
  85.3 47.8 %copy-start.97 = (bf16[24,192]{1,0:T(8,128)(2,1)S(1)}, bf16[24,192]{1,0:T(8,128)(2,1)}, u32[]{:S(2)}) copy-start(bf16[24,192]{1,0:T(8,128)(2,1)} %param.29) | copy-start | bytes 27652
  91.9 60.5 %copy-start.95 = (s32[4096]{0:T(1024)}, s32[4096]{0:T(1024)S(1)}, u32[]{:S(2)}) copy-start(s32[4096]{0:T(1024)S(1)} %broadcast.686) | copy-start | bytes 49156
  107.4 45.0 %copy-start.60 = (s32[5760]{0:T(1024)}, s32[5760]{0:T(1024)S(1)}, u32[]{:S(2)}) copy-start(s32[5760]{0:T(1024)S(1)} %scatter_custom_fusion.1) | copy-start | bytes 69124
  107.5 50.3 %copy-start.82 = (bf16[15,384]{1,0:T(8,128)(2,1)}, bf16[15,384]{1,0:T(8,128)(2,1)S(1)}, u32[]{:S(2)}) copy-start(bf16[15,384]{1,0:T(8,128)(2,1)S(1)} %convert_element_type.214) | copy-start | bytes 34564
  152.9 88.6 %copy-start.9 = (s32[4096]{0:T(1024)}, s32[4096]{0:T(1024)S(1)}, u32[]{:S(2)}) copy-start(s32[4096]{0:T(1024)S(1)} %reshape.1032) | copy-start | bytes 49156
  321.6 33.2 %copy-start.44 = (bf16[1,1024,384]{2,1,0:T(8,128)(2,1)S(1)}, bf16[1,1024,384]{2,1,0:T(8,128)(2,1)}, u32[]{:S(2)}) copy-start(bf16[1,1024,384]{2,1,0:T(8,128)(2,1)} %param.21) | copy-start | bytes 2359300
  321.6 33.5 %copy-start.99 = (s32[1,1024]{1,0:T(1,128)S(1)}, s32[1,1024]{1,0:T(1,128)}, u32[]{:S(2)}) copy-start(s32[1,1024]{1,0:T(1,128)} %param.25) | copy-start | bytes 12292
  321.6 224.8 %all-gather.9.cloned.1.call-start = ((), (), s32[]{:S(2)}) async-start(), calls=%async_computation.9 | async-start | bytes 9400320 | tf_op jit(solution)/shard_map/all_gather | solution.py:175
  322.2 240.0 %all-gather.11.cloned.1.call-start = ((), (), s32[]{:S(2)}) async-start(), calls=%async_computation.10 | async-start | bytes 9400320 | tf_op jit(solution)/shard_map/all_gather | solution.py:176
  322.8 499.5 %all-reduce.10.cloned.1.call-start = ((), (), s32[]{:S(2)}) async-start(), calls=%async_computation.11 | async-start | bytes 1572864 | tf_op jit(solution)/shard_map/psum | solution.py:242
  323.4 134.1 %copy-start.36 = (f32[1,384,15]{2,1,0:T(8,128)}, f32[1,384,15]{2,1,0:T(8,128)S(1)}, u32[]{:S(2)}) copy-start(f32[1,384,15]{2,1,0:T(8,128)S(1)} %copy.301) | copy-start | bytes 69124
  354.9 191.6 %copy-start.45 = (bf16[15,384]{1,0:T(8,128)(2,1)}, bf16[15,384]{1,0:T(8,128)(2,1)S(1)}, u32[]{:S(2)}) copy-start(bf16[15,384]{1,0:T(8,128)(2,1)S(1)} %convert_element_type.223) | copy-start | bytes 34564
  355.2 56.3 %copy-start.29 = (bf16[1,1024,384]{1,2,0:T(8,128)(2,1)}, bf16[1,1024,384]{1,2,0:T(8,128)(2,1)S(1)}, u32[]{:S(2)}) copy-start(bf16[1,1024,384]{1,2,0:T(8,128)(2,1)S(1)} %copy.264) | copy-start | bytes 2359300
  355.2 56.3 %copy-start.80 = (f32[1,1024]{1,0:T(1,128)}, f32[1,1024]{1,0:T(1,128)S(1)}, u32[]{:S(2)}) copy-start(f32[1,1024]{1,0:T(1,128)S(1)} %convert_element_type.230) | copy-start | bytes 12292
  418.2 35.2 %copy-start.61 = (s32[5760]{0:T(1024)S(1)}, s32[5760]{0:T(1024)}, u32[]{:S(2)}) copy-start(s32[5760]{0:T(1024)} %copy-done.60) | copy-start | bytes 69124
  418.2 36.6 %copy-start.77 = (f32[1024]{0:T(1024)S(1)}, f32[1024]{0:T(1024)}, u32[]{:S(2)}) copy-start(f32[1024]{0:T(1024)} %copy-done.76) | copy-start | bytes 12292
  418.3 37.2 %copy-start.16 = (bf16[1,1024,384]{1,2,0:T(8,128)(2,1)S(1)}, bf16[1,1024,384]{1,2,0:T(8,128)(2,1)}, u32[]{:S(2)}) copy-start(bf16[1,1024,384]{1,2,0:T(8,128)(2,1)} %copy-done.15) | copy-start | bytes 2359300
  457.2 39.0 %copy-start.11 = (f32[1,1024,384]{1,2,0:T(8,128)}, f32[1,1024,384]{1,2,0:T(8,128)S(1)}, u32[]{:S(2)}) copy-start(f32[1,1024,384]{1,2,0:T(8,128)S(1)} %get-tuple-element.374) | copy-start | bytes 4718596
  457.2 39.0 %copy-start.58 = (f32[1024]{0:T(1024)}, f32[1024]{0:T(1024)S(1)}, u32[]{:S(2)}) copy-start(f32[1024]{0:T(1024)S(1)} %broadcast_multiply_fusion.4) | copy-start | bytes 12292
  457.5 38.7 %copy-start.67 = (f32[1024]{0:T(1024)}, f32[1024]{0:T(1024)S(1)}, u32[]{:S(2)}) copy-start(f32[1024]{0:T(1024)S(1)} %fusion.185) | copy-start | bytes 12292
  461.0 35.2 %copy-start.7 = (f32[1024,4]{1,0:T(8,128)}, f32[1024,4]{1,0:T(8,128)S(1)}, u32[]{:S(2)}) copy-start(f32[1024,4]{1,0:T(8,128)S(1)} %get-tuple-element.380) | copy-start | bytes 49156
  496.2 176.2 %copy-start.90 = (f32[15,384]{1,0:T(8,128)}, f32[15,384]{1,0:T(8,128)S(1)}, u32[]{:S(2)}) copy-start(f32[15,384]{1,0:T(8,128)S(1)} %mul.382) | copy-start | bytes 69124
  789.5 526.9 %all-reduce.14.cloned.1.call-start = ((), (), s32[]{:S(2)}) async-start(), calls=%async_computation.19 | async-start | bytes 3145728 | tf_op jit(solution)/shard_map/psum | solution.py:222
  799.8 22.5 %copy-start.37 = (f32[1,384,15]{2,1,0:T(8,128)S(1)}, f32[1,384,15]{2,1,0:T(8,128)}, u32[]{:S(2)}) copy-start(f32[1,384,15]{2,1,0:T(8,128)} %copy-done.36) | copy-start | bytes 69124
  803.8 21.4 %copy-start.87 = (f32[1024]{0:T(1024)S(1)}, f32[1024]{0:T(1024)}, u32[]{:S(2)}) copy-start(f32[1024]{0:T(1024)} %copy-done.86) | copy-start | bytes 12292
  806.4 20.1 copy-start.81
  837.5 18.0 copy-start.5
  936.6 11.6 copy-start.2
  1252.6 148.4 %all-reduce.12.cloned.1.call-start = ((), (), s32[]{:S(2)}) async-start(), calls=%async_computation.18 | async-start | bytes 1277952 | tf_op jit(solution)/shard_map/psum | solution.py:294
  1261.9 199.5 %reduce-scatter.11.cloned.1.call-start = ((), (), s32[]{:S(2)}) async-start(), calls=%async_computation.14 | async-start | bytes 417792 | tf_op jit(solution)/shard_map/reduce_scatter | solution.py:289
  1263.1 256.9 %reduce-scatter.9.cloned.1.call-start = ((), (), s32[]{:S(2)}) async-start(), calls=%async_computation.13 | async-start | bytes 417792 | tf_op jit(solution)/shard_map/reduce_scatter | solution.py:288
  1264.3 342.4 %reduce-scatter.13.cloned.1.call-start = ((), (), s32[]{:S(2)}) async-start(), calls=%async_computation.15 | async-start | bytes 6266880 | tf_op jit(solution)/shard_map/reduce_scatter | solution.py:290
  1273.2 419.6 %reduce-scatter.7.cloned.1.call-start = ((), (), s32[]{:S(2)}) async-start(), calls=%async_computation.12 | async-start | bytes 6266880 | tf_op jit(solution)/shard_map/reduce_scatter | solution.py:287
  1281.4 602.2 %reduce-scatter.17.cloned.1.call-start = ((), (), s32[]{:S(2)}) async-start(), calls=%async_computation.17 | async-start | bytes 18800640 | tf_op jit(solution)/shard_map/reduce_scatter | solution.py:292
  1299.9 774.4 %reduce-scatter.15.cloned.1.call-start = ((), (), s32[]{:S(2)}) async-start(), calls=%async_computation.16 | async-start | bytes 18800640 | tf_op jit(solution)/shard_map/reduce_scatter | solution.py:291
  1323.3 754.4 %copy-start.1 = (f32[13,384,15]{1,2,0:T(8,128)S(1)}, f32[13,384,15]{1,2,0:T(8,128)}, u32[]{:S(2)}) copy-start(f32[13,384,15]{1,2,0:T(8,128)} %param.31) | copy-start | bytes 898564
  (77 other events, 358.0 us)
Sparse Core Ops, SparseCore 0:
  10.3 47.4 all-gather.4
  59.9 43.4 all-gather.6
  321.8 49.8 all-reduce.7
  374.1 77.5 all-gather.8
  454.1 75.9 all-gather.10
  789.6 32.6 all-reduce.9
  1252.7 52.5 all-reduce.13
  1310.2 90.6 all-reduce.11
  1405.4 55.9 reduce-scatter.10
  1465.3 54.6 reduce-scatter.8
  1525.0 81.6 reduce-scatter.12
  1611.1 81.6 reduce-scatter.6
  1698.2 185.3 reduce-scatter.16
  1888.8 185.4 reduce-scatter.14
where the time goes:
time: 2100 us; the launch traced here: 2080 us
  waiting for transfers between devices  735 us (35%)
  local copies, waits for them, and re-layouts  721 us (34%)
  matrix products  381 us (18%)
  other arithmetic  120 us (6%)
  blocking collectives  109 us (5%)
    gather x12, local copies, waits for them, and re-layouts, pick_rows(): return jax.vmap(lambda source, index: source[index])(outputs, placed)  277 us
    reduce_scatter x1, waiting for transfers between devices, body(): lax.psum_scatter(grad_down, 'dp', scatter_dimension=2, tiled=True)  191 us
    reduce_scatter x1, waiting for transfers between devices, body(): lax.psum_scatter(grad_up, 'dp', scatter_dimension=1, tiled=True)  191 us
    gather x4, local copies, waits for them, and re-layouts, spread_back(): rows = jax.vmap(lambda source, index: source[index])(grads, patch_ids)  104 us
    gather x4, local copies, waits for them, and re-layouts, dispatch(): rows = jax.vmap(lambda source, index: source[index])(inputs, owners // TOP)  95 us
    reduce_scatter x1, waiting for transfers between devices, body(): lax.psum_scatter(grad_out, 'dp', scatter_dimension=2, tiled=True)  86.7 us
    reduce_scatter x1, waiting for transfers between devices, body(): lax.psum_scatter(grad_query, 'dp', scatter_dimension=1, tiled=True)  86.1 us
    unnamed x216, local copies, waits for them, and re-layouts  80.9 us
  transfers between devices with their start and end apart: 14, of which 8 were waited for; matrix products, arithmetic and copies ran while one was open for 24% of the time, Pallas kernels for 0%

commit v1 on v0

v1 whole, which is shorter than its diff:
```python
import jax
import jax.numpy as jnp
from jax import lax
from jax.experimental import pallas as pl
from jax.experimental.pallas import tpu as pltpu
from jax.sharding import PartitionSpec as P

HDIM = 64
EXPERTS = 15
SLOTS = 16
TOP = 4
CAP = 384
PACK = 16
QT = 256
WIDE = 256

norm_eps = 1e-06
f32 = jnp.float32
bf16 = jnp.bfloat16
highest = lax.Precision.HIGHEST
log2e = 1.4426950408889634
score_scale = 0.125 * log2e
vmem_bytes = 56 * 1024 * 1024


def nn(a, b):
    return jnp.dot(a, b, preferred_element_type=f32)


def nt(a, b):
    return lax.dot_general(a, b, (((1,), (1,)), ((), ())), preferred_element_type=f32)


def params(limit=vmem_bytes):
    return pltpu.CompilerParams(vmem_limit_bytes=limit)


def cost(flops, moved):
    return pl.CostEstimate(flops=int(flops), bytes_accessed=int(moved), transcendentals=0)


def vspec():
    return pl.BlockSpec(memory_space=pltpu.VMEM)


def sds(shape, dtype):
    return jax.ShapeDtypeStruct(shape, dtype)


def norm_stats(x):
    centre = jnp.mean(x, axis=-1, keepdims=True)
    shifted = x - centre
    spread = jnp.mean(shifted * shifted, axis=-1, keepdims=True)
    inv = lax.rsqrt(spread + norm_eps)
    return shifted * inv, inv


def dense_gates(logits, chosen):
    top = jnp.max(jnp.where(chosen, logits, -jnp.inf), axis=0, keepdims=True)
    lifted = jnp.where(chosen, jnp.exp(logits - top), 0.0)
    return lifted / jnp.sum(lifted, axis=0, keepdims=True)


def prep_kernel(tok_ref, gain_ref, router_ref, ra_ref, rm_ref, x_ref, gate_ref, cma_ref, cmm_ref, meta_ref):
    patches = tok_ref.shape[0]
    xhat, _ = norm_stats(tok_ref[...].astype(f32))
    normed = xhat * gain_ref[...]
    x_ref[...] = normed.astype(bf16)
    ids = lax.broadcasted_iota(jnp.int32, (SLOTS, patches), 0)
    before = (
        lax.broadcasted_iota(jnp.int32, (patches, patches), 0)
        < lax.broadcasted_iota(jnp.int32, (patches, patches), 1)
    )
    tri = jnp.where(before, 1.0, 0.0).astype(bf16)
    small = lax.broadcasted_iota(jnp.int32, (SLOTS, SLOTS), 1) < lax.broadcasted_iota(
        jnp.int32, (SLOTS, SLOTS), 0
    )
    lower = jnp.where(small, 1.0, 0.0)
    for routes, cm_ref, at in ((ra_ref, cma_ref, 0), (rm_ref, cmm_ref, 2)):
        named = jnp.zeros((SLOTS, patches), f32)
        for k in range(TOP):
            named = named + jnp.where(routes[k : k + 1, :] == ids, 1.0, 0.0)
        ranks = nn(named.astype(bf16), tri)
        cm_ref[...] = jnp.where(named > 0.0, ranks, -1.0).astype(jnp.int32)
        count = jnp.sum(named, axis=1, keepdims=True)
        packed = jnp.ceil(count * (1.0 / PACK)) * PACK
        packed = jnp.broadcast_to(packed, (SLOTS, 128))
        offs = jnp.dot(lower, packed, precision=highest, preferred_element_type=f32)
        meta_ref[at] = offs.astype(jnp.int32)
        meta_ref[at + 1] = jnp.broadcast_to(count, (SLOTS, 128)).astype(jnp.int32)
    logits = lax.dot_general(
        router_ref[...], normed, (((1,), (1,)), ((), ())), precision=highest, preferred_element_type=f32
    )
    gate_ref[...] = dense_gates(logits, cma_ref[...] >= 0)


def prep(tokens, gain, router_t, ra_t, rm_t):
    patches, width = tokens.shape
    return pl.pallas_call(
        prep_kernel,
        out_shape=(
            sds((patches, width), bf16),
            sds((SLOTS, patches), f32),
            sds((SLOTS, patches), jnp.int32),
            sds((SLOTS, patches), jnp.int32),
            sds((4, SLOTS, 128), jnp.int32),
        ),
        in_specs=[vspec()] * 5,
        out_specs=[vspec()] * 5,
        compiler_params=params(),
        cost_estimate=cost(8e9, 4e6),
        name="prep",
    )(tokens, gain, router_t, ra_t, rm_t)


def one_hot(cm_row, rows):
    return cm_row == lax.broadcasted_iota(jnp.int32, (rows, cm_row.shape[1]), 0)


def masks(heads):
    lane = lax.broadcasted_iota(jnp.int32, (1, WIDE), 1)
    return [(lane >= h * HDIM) & (lane < (h + 1) * HDIM) for h in range(heads)], lane


def attend_kernel(
    meta, x_ref, cm_ref, wq_ref, wk_ref, wv_ref, o_ref, q_ref, lse_ref, k_ref, v_ref, rows_ref, km, vm
):
    heads = km.shape[0]
    local = heads * HDIM
    x = x_ref[...]
    head_mask, lane = masks(heads)
    k = nn(x, wk_ref[...]).astype(bf16)
    v = nn(x, wv_ref[...]).astype(bf16)
    k_ref[...] = k
    v_ref[...] = v
    for h in range(heads):
        km[h] = jnp.where(head_mask[h], k.astype(f32), 0.0).astype(bf16)
        ones = jnp.where(lane == local + h, 1.0, 0.0)
        vm[h] = jnp.where(head_mask[h], v.astype(f32), ones).astype(bf16)
    q_ref[...] = jnp.zeros(q_ref.shape, bf16)

    def project(e, carry):
        off = pl.multiple_of(meta[0, e], PACK)
        hot = jnp.where(one_hot(cm_ref[pl.ds(e, 1), :], CAP), 1.0, 0.0).astype(bf16)
        rows = nn(hot, x).astype(bf16)
        rows_ref[e] = rows
        q_ref[pl.ds(off, CAP), :local] = nn(rows, wq_ref[e]).astype(bf16)
        return carry

    lax.fori_loop(0, EXPERTS, project, 0)
    tiles = (meta[0, EXPERTS] + (QT - 1)) // QT

    def tile(i, carry):
        start = pl.multiple_of(i * QT, QT)
        q = q_ref[pl.ds(start, QT), :]
        out = jnp.zeros((QT, WIDE), f32)
        stats = jnp.zeros((QT, 128), f32)
        lane_s = lax.broadcasted_iota(jnp.int32, (1, 128), 1)
        for h in range(heads):
            s = nt(q, km[h])
            top = jnp.max(s, axis=1, keepdims=True) * score_scale
            p = jnp.exp2(s * score_scale - top).astype(bf16)
            oh = nn(p, vm[h])
            total = oh[:, local + h : local + h + 1]
            out = jnp.where(head_mask[h], oh * (1.0 / total), out)
            stats = jnp.where(lane_s == h, top + jnp.log2(total), stats)
        o_ref[pl.ds(start, QT), :] = out.astype(bf16)
        lse_ref[pl.ds(start, QT), :] = stats
        return carry

    o_ref[...] = jnp.zeros(o_ref.shape, bf16)
    lax.fori_loop(0, tiles, tile, 0)


def packed_rows(patches):
    return -(-(patches * TOP + EXPERTS * PACK + CAP) // QT) * QT


def attend(meta, x, cm, wq, wk, wv):
    patches, width = x.shape
    heads = wq.shape[2] // HDIM
    rows = packed_rows(patches)
    return pl.pallas_call(
        attend_kernel,
        out_shape=(
            sds((rows, WIDE), bf16),
            sds((rows, WIDE), bf16),
            sds((rows, 128), f32),
            sds((patches, WIDE), bf16),
            sds((patches, WIDE), bf16),
            sds((EXPERTS, CAP, width), bf16),
        ),
        in_specs=[pl.BlockSpec(memory_space=pltpu.SMEM)] + [vspec()] * 5,
        out_specs=[vspec()] * 6,
        scratch_shapes=[pltpu.VMEM((heads, patches, WIDE), bf16), pltpu.VMEM((heads, patches, WIDE), bf16)],
        compiler_params=params(),
        cost_estimate=cost(30e9, 2e7),
        name="attend",
    )(meta, x, cm, wq, wk, wv)


def out_kernel(meta, o_ref, cm_ref, gate_ref, wo_ref, part_ref, acc):
    local = wo_ref.shape[2]
    acc[...] = jnp.zeros(acc.shape, f32)

    def expert(e, carry):
        off = pl.multiple_of(meta[0, e], PACK)
        mixed = o_ref[pl.ds(off, CAP), :local]
        outs = nt(wo_ref[e], mixed).astype(bf16)
        hot = one_hot(cm_ref[pl.ds(e, 1), :], CAP)
        gated = jnp.where(hot, gate_ref[pl.ds(e, 1), :], 0.0).astype(bf16)
        acc[...] += nn(outs, gated)
        return carry

    lax.fori_loop(0, EXPERTS, expert, 0)
    part_ref[...] = acc[...].T.astype(bf16)


def out_project(meta, o, cm, gates, wo_t):
    patches = cm.shape[1]
    width = wo_t.shape[1]
    return pl.pallas_call(
        out_kernel,
        out_shape=sds((patches, width), bf16),
        in_specs=[pl.BlockSpec(memory_space=pltpu.SMEM)] + [vspec()] * 4,
        out_specs=vspec(),
        scratch_shapes=[pltpu.VMEM((width, patches), f32)],
        compiler_params=params(),
        cost_estimate=cost(8e9, 8e6),
        name="out_project",
    )(meta, o, cm, gates, wo_t)


def middle_kernel(tok_ref, mine_ref, other_ref, gain_ref, router_ref, cm_ref, grad_ref, mid_ref, x_ref, gate_ref):
    width = tok_ref.shape[1]
    middle = tok_ref[...].astype(f32) + (mine_ref[...].astype(f32) + other_ref[...].astype(f32))
    mid_ref[...] = middle
    xhat, _ = norm_stats(middle)
    normed = xhat * gain_ref[...]
    x_ref[:, :width] = normed.astype(bf16)
    x_ref[:, width:] = grad_ref[...]
    logits = lax.dot_general(
        router_ref[...], normed, (((1,), (1,)), ((), ())), precision=highest, preferred_element_type=f32
    )
    gate_ref[...] = dense_gates(logits, cm_ref[...] >= 0)


def middle_step(tokens, mine, other, gain, router_t, cm, masked):
    patches, width = tokens.shape
    return pl.pallas_call(
        middle_kernel,
        out_shape=(
            sds((patches, width), f32),
            sds((patches, 2 * width), bf16),
            sds((SLOTS, patches), f32),
        ),
        in_specs=[vspec()] * 7,
        out_specs=[vspec()] * 3,
        compiler_params=params(),
        cost_estimate=cost(4e9, 6e6),
        name="middle",
    )(tokens, mine, other, gain, router_t, cm, masked)


def gelu_parts(x):
    c = 0.7978845608028654
    square = x * x
    t = jnp.tanh(x * (c + (c * 0.044715) * square))
    half = 0.5 * (1.0 + t)
    slope = half + (0.5 * x) * (1.0 - t * t) * (c + (3.0 * c * 0.044715) * square)
    return x * half, slope


def feed_kernel(meta, x_ref, cm_ref, gate_ref, up_ref, down_ref, grad_ref, part_ref, gg_ref, acc):
    e = pl.program_id(0)
    width = x_ref.shape[1] // 2

    @pl.when(e == 0)
    def _():
        acc[...] = jnp.zeros(acc.shape, f32)
        gg_ref[...] = jnp.zeros(gg_ref.shape, f32)

    def work(rows_n):
        eq = one_hot(cm_ref[pl.ds(e, 1), :], rows_n)
        hot = jnp.where(eq, 1.0, 0.0).astype(bf16)
        gsel = jnp.where(eq, gate_ref[pl.ds(e, 1), :], 0.0)
        grow = jnp.sum(gsel, axis=1, keepdims=True)
        gated = gsel.astype(bf16)
        got = nn(hot, x_ref[...])
        rows = got[:, :width]
        grads = got[:, width:]
        up = up_ref[0]
        down = down_ref[0]
        hidden = nn(rows.astype(bf16), up)
        act, slope = gelu_parts(hidden)
        acts = act.astype(bf16)
        raw = nn(grads.astype(bf16), down)
        gg = jnp.sum(raw * acts.astype(f32), axis=1, keepdims=True)
        gg_ref[pl.ds(e, 1), :] = jnp.sum(jnp.where(eq, gg, 0.0), axis=0, keepdims=True)
        hidden_grad = (raw * grow * slope).astype(bf16)
        out_grad = (grads * grow).T.astype(bf16)
        grad_ref[1, 0] = nn(out_grad, acts).astype(bf16)
        grad_ref[0, 0] = nn(rows.T.astype(bf16), hidden_grad).astype(bf16)
        outs = nt(down, acts).astype(bf16)
        acc[:width] += nn(outs, gated)
        back = nt(up, hidden_grad).astype(bf16)
        acc[width:] += nn(back, hot)

    few = meta[1, e] <= 256

    @pl.when(few)
    def _():
        work(256)

    @pl.when(jnp.logical_not(few))
    def _():
        work(CAP)

    @pl.when(e == EXPERTS - 1)
    def _():
        part_ref[0] = acc[:width].T.astype(bf16)
        part_ref[1] = acc[width:].T.astype(bf16)


def feed(meta, x, cm, gates, weights):
    patches, double = x.shape
    width = double // 2
    hidden = weights.shape[2]
    return pl.pallas_call(
        feed_kernel,
        out_shape=(
            sds((2, EXPERTS, width, hidden), bf16),
            sds((2, patches, width), bf16),
            sds((SLOTS, patches), f32),
        ),
        grid_spec=pltpu.PrefetchScalarGridSpec(
            num_scalar_prefetch=1,
            grid=(EXPERTS,),
            in_specs=[
                pl.BlockSpec((patches, double), lambda e, m: (0, 0)),
                pl.BlockSpec((SLOTS, patches), lambda e, m: (0, 0)),
                pl.BlockSpec((SLOTS, patches), lambda e, m: (0, 0)),
                pl.BlockSpec((1, width, hidden), lambda e, m: (e, 0, 0)),
                pl.BlockSpec((1, width, hidden), lambda e, m: (e + EXPERTS, 0, 0)),
            ],
            out_specs=[
                pl.BlockSpec((2, 1, width, hidden), lambda e, m: (0, e, 0, 0)),
                pl.BlockSpec((2, patches, width), lambda e, m: (0, 0, 0)),
                pl.BlockSpec((SLOTS, patches), lambda e, m: (0, 0)),
            ],
            scratch_shapes=[pltpu.VMEM((double, patches), f32)],
        ),
        compiler_params=params(),
        cost_estimate=cost(38e9, 4e7),
        name="feed",
    )(meta, x, cm, gates, weights, weights)


def gate_back(gates, gg):
    return gates * (gg - jnp.sum(gates * gg, axis=0, keepdims=True))


def norm_back(xhat, inv, grad, gain):
    lifted = grad * gain
    first = jnp.mean(lifted, axis=-1, keepdims=True)
    second = jnp.mean(lifted * xhat, axis=-1, keepdims=True)
    return inv * (lifted - first - xhat * second)


def tn_high(a, b):
    return lax.dot_general(a, b, (((0,), (0,)), ((), ())), precision=highest, preferred_element_type=f32)


def second_back_kernel(
    mid_ref, mine_ref, other_ref, ggm_ref, ggo_ref, gate_ref, router_ref, gain_ref, masked_ref,
    mg_ref, mgb_ref, groute_ref, ggain_ref,
):
    xhat, inv = norm_stats(mid_ref[...])
    logit_grad = gate_back(gate_ref[...], ggm_ref[...] + ggo_ref[...])
    grad = (mine_ref[...].astype(f32) + other_ref[...].astype(f32)) + tn_high(logit_grad, router_ref[...])
    groute_ref[...] = jnp.dot(
        logit_grad, xhat * gain_ref[...], precision=highest, preferred_element_type=f32
    )
    ggain_ref[...] = jnp.sum(grad * xhat, axis=0, keepdims=True)
    middle_grad = masked_ref[...].astype(f32) + norm_back(xhat, inv, grad, gain_ref[...])
    mg_ref[...] = middle_grad
    mgb_ref[...] = middle_grad.astype(bf16)


def second_back(middle, mine, other, gg_mine, gg_other, gates, router_t, gain, masked):
    patches, width = middle.shape
    return pl.pallas_call(
        second_back_kernel,
        out_shape=(
            sds((patches, width), f32),
            sds((patches, width), bf16),
            sds((SLOTS, width), f32),
            sds((1, width), f32),
        ),
        in_specs=[vspec()] * 9,
        out_specs=[vspec()] * 4,
        compiler_params=params(),
        cost_estimate=cost(4e9, 8e6),
        name="second_back",
    )(middle, mine, other, gg_mine, gg_other, gates, router_t, gain, masked)


def out_back_kernel(meta, mg_ref, cm_ref, gate_ref, wo_ref, o_ref, do_ref, delta_ref, gg_ref, grad_ref):
    e = pl.program_id(0)
    local = wo_ref.shape[2]

    @pl.when(e == 0)
    def _():
        do_ref[...] = jnp.zeros(do_ref.shape, bf16)
        delta_ref[...] = jnp.zeros(delta_ref.shape, f32)
        gg_ref[...] = jnp.zeros(gg_ref.shape, f32)

    off = pl.multiple_of(meta[0, e], PACK)
    eq = one_hot(cm_ref[pl.ds(e, 1), :], CAP)
    hot = jnp.where(eq, 1.0, 0.0).astype(bf16)
    grow = jnp.sum(jnp.where(eq, gate_ref[pl.ds(e, 1), :], 0.0), axis=1, keepdims=True)
    grads = nn(hot, mg_ref[...])
    mixed = o_ref[pl.ds(off, CAP), :local]
    mixed_f = mixed.astype(f32)
    raw = nn(grads.astype(bf16), wo_ref[0])
    gg = jnp.sum(raw * mixed_f, axis=1, keepdims=True)
    gg_ref[pl.ds(e, 1), :] = jnp.sum(jnp.where(eq, gg, 0.0), axis=0, keepdims=True)
    mixed_grad = (raw * grow).astype(bf16)
    do_ref[pl.ds(off, CAP), :local] = mixed_grad
    weighed = mixed_grad.astype(f32) * mixed_f
    lane = lax.broadcasted_iota(jnp.int32, (1, local), 1)
    lane_s = lax.broadcasted_iota(jnp.int32, (1, 128), 1)
    delta = jnp.zeros((CAP, 128), f32)
    for h in range(local // HDIM):
        here = (lane >= h * HDIM) & (lane < (h + 1) * HDIM)
        total = jnp.sum(jnp.where(here, weighed, 0.0), axis=1, keepdims=True)
        delta = jnp.where(lane_s == h, total, delta)
    delta_ref[pl.ds(off, CAP), :] = delta
    grad_ref[0] = nn((grads * grow).T.astype(bf16), mixed).astype(bf16)


def out_back(meta, mg, cm, gates, wo_t, o):
    patches, width = mg.shape
    local = wo_t.shape[2]
    rows = o.shape[0]
    return pl.pallas_call(
        out_back_kernel,
        out_shape=(
            sds((rows, WIDE), bf16),
            sds((rows, 128), f32),
            sds((SLOTS, patches), f32),
            sds((EXPERTS, width, local), bf16),
        ),
        grid_spec=pltpu.PrefetchScalarGridSpec(
            num_scalar_prefetch=1,
            grid=(EXPERTS,),
            in_specs=[
                pl.BlockSpec((patches, width), lambda e, m: (0, 0)),
                pl.BlockSpec((SLOTS, patches), lambda e, m: (0, 0)),
                pl.BlockSpec((SLOTS, patches), lambda e, m: (0, 0)),
                pl.BlockSpec((1, width, local), lambda e, m: (e, 0, 0)),
                pl.BlockSpec((rows, WIDE), lambda e, m: (0, 0)),
            ],
            out_specs=[
                pl.BlockSpec((rows, WIDE), lambda e, m: (0, 0)),
                pl.BlockSpec((rows, 128), lambda e, m: (0, 0)),
                pl.BlockSpec((SLOTS, patches), lambda e, m: (0, 0)),
                pl.BlockSpec((1, width, local), lambda e, m: (e, 0, 0)),
            ],
        ),
        compiler_params=params(),
        cost_estimate=cost(10e9, 2e7),
        name="out_back",
    )(meta, mg, cm, gates, wo_t, o)


def attend_back_kernel(meta, q_ref, do_ref, lse_ref, delta_ref, k_ref, v_ref, dq_ref, dk_ref, dv_ref, km, vm, dk, dv):
    heads = km.shape[0]
    head_mask, _ = masks(heads)
    k = k_ref[...].astype(f32)
    v = v_ref[...].astype(f32)
    for h in range(heads):
        km[h] = jnp.where(head_mask[h], k, 0.0).astype(bf16)
        vm[h] = jnp.where(head_mask[h], v, 0.0).astype(bf16)
    dk[...] = jnp.zeros(dk.shape, f32)
    dv[...] = jnp.zeros(dv.shape, f32)
    dq_ref[...] = jnp.zeros(dq_ref.shape, bf16)
    tiles = (meta[0, EXPERTS] + (QT - 1)) // QT

    def tile(i, carry):
        start = pl.multiple_of(i * QT, QT)
        q = q_ref[pl.ds(start, QT), :]
        do = do_ref[pl.ds(start, QT), :]
        lse = lse_ref[pl.ds(start, QT), :]
        delta = delta_ref[pl.ds(start, QT), :]
        q_t = q.astype(f32).T.astype(bf16)
        do_t = do.astype(f32).T.astype(bf16)
        dq = jnp.zeros((QT, WIDE), f32)
        for h in range(heads):
            at = slice(h * HDIM, (h + 1) * HDIM)
            s = nt(q, km[h])
            p = jnp.exp2(s * score_scale - lse[:, h : h + 1])
            dp = nt(do, vm[h])
            ds = (p * (dp - delta[:, h : h + 1])).astype(bf16)
            dq = dq + nn(ds, km[h])
            dk[at, :] += nn(q_t[at, :], ds)
            dv[at, :] += nn(do_t[at, :], p.astype(bf16))
        dq_ref[pl.ds(start, QT), :] = (dq * 0.125).astype(bf16)
        return carry

    lax.fori_loop(0, tiles, tile, 0)
    dk_ref[...] = (dk[...] * 0.125).astype(bf16)
    dv_ref[...] = dv[...].astype(bf16)


def attend_back(meta, q, do, lse, delta, k, v, heads):
    rows = q.shape[0]
    patches = k.shape[0]
    return pl.pallas_call(
        attend_back_kernel,
        out_shape=(
            sds((rows, WIDE), bf16),
            sds((heads * HDIM, patches), bf16),
            sds((heads * HDIM, patches), bf16),
        ),
        in_specs=[pl.BlockSpec(memory_space=pltpu.SMEM)] + [vspec()] * 6,
        out_specs=[vspec()] * 3,
        scratch_shapes=[
            pltpu.VMEM((heads, patches, WIDE), bf16),
            pltpu.VMEM((heads, patches, WIDE), bf16),
            pltpu.VMEM((heads * HDIM, patches), f32),
            pltpu.VMEM((heads * HDIM, patches), f32),
        ],
        compiler_params=params(),
        cost_estimate=cost(60e9, 2e7),
        name="attend_back",
    )(meta, q, do, lse, delta, k, v)


def in_back_kernel(meta, dq_ref, dk_ref, dv_ref, rows_ref, x_ref, cm_ref, wq_ref, wk_ref, wv_ref, grad_ref, part_ref, acc):
    e = pl.program_id(0)
    local = wq_ref.shape[2]

    @pl.when(e == 0)
    def _():
        dk = dk_ref[...]
        dv = dv_ref[...]
        acc[...] = nn(wk_ref[...], dk) + nn(wv_ref[...], dv)

    off = pl.multiple_of(meta[0, e], PACK)

    @pl.when(e < EXPERTS)
    def _():
        dq = dq_ref[pl.ds(off, CAP), :local]
        rows_t = rows_ref[0].astype(f32).T.astype(bf16)
        grad_ref[0] = nn(rows_t, dq).astype(bf16)
        back = nt(wq_ref[0], dq).astype(bf16)
        hot = jnp.where(one_hot(cm_ref[pl.ds(e, 1), :], CAP), 1.0, 0.0).astype(bf16)
        acc[...] += nn(back, hot)

    @pl.when(e == EXPERTS)
    def _():
        part_ref[...] = acc[...].T.astype(bf16)
        grad_ref[0] = nn(dk_ref[...], x_ref[...]).T.astype(bf16)

    @pl.when(e == EXPERTS + 1)
    def _():
        grad_ref[0] = nn(dv_ref[...], x_ref[...]).T.astype(bf16)


def in_back(meta, dq, dk, dv, rows_att, x, cm, wq, wk, wv):
    patches, width = x.shape
    local = wq.shape[2]
    rows = dq.shape[0]
    top = EXPERTS - 1
    return pl.pallas_call(
        in_back_kernel,
        out_shape=(sds((EXPERTS + 2, width, local), bf16), sds((patches, width), bf16)),
        grid_spec=pltpu.PrefetchScalarGridSpec(
            num_scalar_prefetch=1,
            grid=(EXPERTS + 2,),
            in_specs=[
                pl.BlockSpec((rows, WIDE), lambda e, m: (0, 0)),
                pl.BlockSpec((local, patches), lambda e, m: (0, 0)),
                pl.BlockSpec((local, patches), lambda e, m: (0, 0)),
                pl.BlockSpec((1, CAP, width), lambda e, m: (jnp.minimum(e, top), 0, 0)),
                pl.BlockSpec((patches, width), lambda e, m: (0, 0)),
                pl.BlockSpec((SLOTS, patches), lambda e, m: (0, 0)),
                pl.BlockSpec((1, width, local), lambda e, m: (jnp.minimum(e, top), 0, 0)),
                pl.BlockSpec((width, local), lambda e, m: (0, 0)),
                pl.BlockSpec((width, local), lambda e, m: (0, 0)),
            ],
            out_specs=[
                pl.BlockSpec((1, width, local), lambda e, m: (e, 0, 0)),
                pl.BlockSpec((patches, width), lambda e, m: (0, 0)),
            ],
            scratch_shapes=[pltpu.VMEM((width, patches), f32)],
        ),
        compiler_params=params(),
        cost_estimate=cost(10e9, 2e7),
        name="in_back",
    )(meta, dq, dk, dv, rows_att, x, cm, wq, wk, wv)


def route_back_kernel(tok_ref, ggm_ref, ggo_ref, gate_ref, gain_ref, lg_ref, groute_ref):
    xhat, _ = norm_stats(tok_ref[...].astype(f32))
    logit_grad = gate_back(gate_ref[...], ggm_ref[...] + ggo_ref[...])
    lg_ref[...] = logit_grad
    groute_ref[...] = jnp.dot(
        logit_grad, xhat * gain_ref[...], precision=highest, preferred_element_type=f32
    )


def route_back(tokens, gg_mine, gg_other, gates, gain):
    patches, width = tokens.shape
    return pl.pallas_call(
        route_back_kernel,
        out_shape=(sds((SLOTS, patches), f32), sds((SLOTS, width), f32)),
        in_specs=[vspec()] * 5,
        out_specs=[vspec()] * 2,
        compiler_params=params(),
        cost_estimate=cost(3e9, 2e6),
        name="route_back",
    )(tokens, gg_mine, gg_other, gates, gain)


def first_back_kernel(tok_ref, mine_ref, other_ref, lg_ref, router_ref, gain_ref, mg_ref, gt_ref, ggain_ref):
    xhat, inv = norm_stats(tok_ref[...].astype(f32))
    grad = (mine_ref[...].astype(f32) + other_ref[...].astype(f32)) + tn_high(lg_ref[...], router_ref[...])
    ggain_ref[...] = jnp.sum(grad * xhat, axis=0, keepdims=True)
    gt_ref[...] = mg_ref[...] + norm_back(xhat, inv, grad, gain_ref[...])


def first_back(tokens, mine, other, logit_grad, router_t, gain, middle_grad):
    patches, width = tokens.shape
    return pl.pallas_call(
        first_back_kernel,
        out_shape=(sds((patches, width), f32), sds((1, width), f32)),
        in_specs=[vspec()] * 7,
        out_specs=[vspec()] * 2,
        compiler_params=params(),
        cost_estimate=cost(3e9, 6e6),
        name="first_back",
    )(tokens, mine, other, logit_grad, router_t, gain, middle_grad)


def other_half(x):
    return lax.ppermute(x, "mp", [(0, 1), (1, 0)])


def cube_steps(size):
    steps = []
    step = 1
    while step < size:
        steps.append(step)
        step *= 2
    return steps


def cube_sum(x, size):
    for step in cube_steps(size):
        x = x + lax.ppermute(x, "dp", [(i, i ^ step) for i in range(size)])
    return x


def cube_gather(x, size):
    index = lax.axis_index("dp")
    x = x[None]
    for step in cube_steps(size):
        got = lax.ppermute(x, "dp", [(i, i ^ step) for i in range(size)])
        upper = (index // step) % 2 == 1
        x = jnp.where(
            upper, jnp.concatenate([got, x], axis=0), jnp.concatenate([x, got], axis=0)
        )
    return x


def body(dp_size, tokens, cotangent, task_ids, att_routes, mlp_routes, valid, gain_one, w_query, w_key,
         w_value, w_out, router_att, gain_two, w_up, w_down, router_mlp):
    tokens = tokens[0]
    patches, width = tokens.shape
    local = w_key.shape[1]
    heads = local // HDIM
    tasks = router_att.shape[0]

    att_shard = jnp.concatenate([w_query, jnp.swapaxes(w_out, 1, 2), w_key[None], w_value[None]], axis=0)
    feed_shard = jnp.concatenate([w_up, jnp.swapaxes(w_down, 1, 2)], axis=0)
    att_full = lax.all_gather(att_shard, "dp", axis=1, tiled=True)
    feed_full = lax.all_gather(feed_shard, "dp", axis=1, tiled=True)

    gain_1 = gain_one[None]
    gain_2 = gain_two[None]
    task = task_ids[0]
    pick = lambda router: jnp.pad(
        lax.dynamic_index_in_dim(router, task, 0, keepdims=False).T, ((0, SLOTS - EXPERTS), (0, 0))
    )
    route_1 = pick(router_att)
    route_2 = pick(router_mlp)
    masked = cotangent[0] * valid[0][:, None].astype(bf16)

    x_one, gates_1, cm_1, cm_2, meta = prep(tokens, gain_1, route_1, att_routes[0].T, mlp_routes[0].T)
    meta_1 = meta[0:2, :, 0]
    meta_2 = meta[2:4, :, 0]

    wq = att_full[:EXPERTS]
    wo_t = att_full[EXPERTS : 2 * EXPERTS]
    wk = att_full[2 * EXPERTS]
    wv = att_full[2 * EXPERTS + 1]
    grow = ((0, 0), (0, WIDE - local))
    o, q, lse, k, v, rows_att = attend(meta_1, x_one, cm_1, wq, jnp.pad(wk, grow), jnp.pad(wv, grow))
    part = out_project(meta_1, o, cm_1, gates_1, wo_t)
    middle, x_two, gates_2 = middle_step(tokens, part, other_half(part), gain_2, route_2, cm_2, masked)
    feed_grads, parts, gg_2 = feed(meta_2, x_two, cm_2, gates_2, feed_full)
    back_two = parts[1]
    middle_grad, mg, groute_2, ggain_2 = second_back(
        middle, back_two, other_half(back_two), gg_2, other_half(gg_2), gates_2, route_2, gain_2, masked
    )
    layer_out = (middle + (parts[0].astype(f32) + other_half(parts[0]).astype(f32))).astype(bf16)
    do, delta, gg_1, grad_out = out_back(meta_1, mg, cm_1, gates_1, wo_t, o)
    logit_grad, groute_1 = route_back(tokens, gg_1, other_half(gg_1), gates_1, gain_1)
    dq, dk, dv = attend_back(meta_1, q, do, lse, delta, k, v, heads)
    grad_in, back_one = in_back(meta_1, dq, dk, dv, rows_att, x_one, cm_1, wq, wk, wv)
    grad_tokens, ggain_1 = first_back(
        tokens, back_one, other_half(back_one), logit_grad, route_1, gain_1, middle_grad
    )

    scatter = lambda g: lax.psum_scatter(g, "dp", scatter_dimension=1, tiled=True).astype(f32)
    feed_mine = scatter(feed_grads.reshape(2 * EXPERTS, width, w_up.shape[2]))
    out_mine = scatter(grad_out)
    in_mine = scatter(grad_in)

    mark = (jnp.arange(width) == task).astype(f32)[None]
    small = jnp.concatenate([groute_1[:EXPERTS], mark, groute_2[:EXPERTS], ggain_2], axis=0)
    every = cube_gather(small, dp_size)
    marks = every[:, EXPERTS, :tasks]
    route_sum = lambda g: jnp.swapaxes(
        jnp.einsum("it,ied->ted", marks, g, precision=highest, preferred_element_type=f32), 1, 2
    )
    grad_router_att = route_sum(every[:, :EXPERTS])
    grad_router_mlp = route_sum(every[:, SLOTS : SLOTS + EXPERTS])
    grad_gain_two = jnp.sum(every[:, 2 * SLOTS - 1], axis=0)
    grad_gain_one = cube_sum(ggain_1, dp_size)[0]
    return (
        layer_out[None],
        grad_tokens[None],
        grad_gain_one,
        in_mine[:EXPERTS],
        in_mine[EXPERTS],
        in_mine[EXPERTS + 1],
        jnp.swapaxes(out_mine, 1, 2),
        grad_router_att,
        grad_gain_two,
        feed_mine[:EXPERTS],
        jnp.swapaxes(feed_mine[EXPERTS:], 1, 2),
        grad_router_mlp,
    )


def solution(mesh):
    dp_size = mesh.shape["dp"]

    def run(*args):
        return body(dp_size, *args)

    return jax.shard_map(
        run,
        mesh=mesh,
        in_specs=(
            P("dp", None, None), P("dp", None, None), P("dp"), P("dp", None, None), P("dp", None, None),
            P("dp", None), P(), P(None, "dp", "mp"), P("dp", "mp"), P("dp", "mp"), P(None, "mp", "dp"),
            P(), P(), P(None, "dp", "mp"), P(None, "mp", "dp"), P(),
        ),
        out_specs=(
            P("dp", None, None), P("dp", None, None), P(), P(None, "dp", "mp"), P("dp", "mp"), P("dp", "mp"),
            P(None, "mp", "dp"), P(), P(), P(None, "dp", "mp"), P(None, "mp", "dp"), P(),
        ),
        check_vma=False,
    )
```

time: 2100 us -> 669 us (0.32)
  local copies, waits for them, and re-layouts: 721 us -> 58.4 us
  waiting for transfers between devices: 735 us -> 325 us
  matrix products: 381 us -> 1.09 us
  Pallas kernels: 0 us -> 235 us
  blocking collectives: 109 us -> 0 us
  other arithmetic: 120 us -> 13.9 us
    reduce_scatter x6 -> x0, waiting for transfers between devices: 673 us -> none  [the longest x1 191 us: body(): lax.psum_scatter(grad_down, 'dp', scatter_dimension=2, tiled=True)]
    gather x24 -> x0, local copies, waits for them, and re-layouts: 547 us -> none  [the longest x12 277 us: pick_rows(): return jax.vmap(lambda source, index: source[index])(outputs, placed)]
    dot_general x67 -> x2, matrix products: 381 us -> 1.09 us  [body(): jnp.einsum('it,ied->ted', marks, g, precision=highest, preferred_element_...]
    pallas_call x0 -> x11, Pallas kernels: none -> 235 us  [the longest x1 58.2 us: feed(): pl.pallas_call(feed_kernel, out_shape=(sds((2, EXPERTS, width, hidden), b...]
    unnamed x14 -> x8, waiting for transfers between devices: 2.6 us -> 193 us
    ppermute x0 -> x14, waiting for transfers between devices: none -> 75.3 us  [the longest x6 51.5 us: other_half(): return lax.ppermute(x, 'mp', [(0, 1), (1, 0)])]
    psum x3 -> x0, blocking collectives: 67.5 us -> none  [the longest x1 31.7 us: body(): lax.psum((grad_gain_one, grad_router_att, grad_gain_two, grad_router_mlp)...]
    convert_element_type x13 -> x4, other arithmetic: 60.8 us -> 0.72 us  [the longest x2 0.69 us: body(): lax.psum_scatter(g, 'dp', scatter_dimension=1, tiled=True).astype(f32)]
  transfers between devices with their start and end apart: 14 -> 19, of which waited for: 8 -> 11; matrix products, arithmetic and copies ran while one was open for 24% -> 9% of each run, Pallas kernels for 0% -> 22%
where the time goes in v1:
time: 669 us; the launch traced here: 663 us
  waiting for transfers between devices  325 us (49%)
  Pallas kernels  235 us (35%)
  local copies, waits for them, and re-layouts  58.4 us (9%)
  between operations  15.8 us (2%)
  starting transfers between devices  14.5 us (2%)
  other arithmetic  13.9 us (2%)
    unnamed x8, waiting for transfers between devices  193 us
    pallas_call x1, Pallas kernels, feed(): pl.pallas_call(feed_kernel, out_shape=(sds((2, EXPERTS, width, hidden), b...  58.2 us
    all_gather x1, waiting for transfers between devices, body(): att_full = lax.all_gather(att_shard, 'dp', axis=1, tiled=True)  56.7 us
    ppermute x6, waiting for transfers between devices, other_half(): return lax.ppermute(x, 'mp', [(0, 1), (1, 0)])  51.5 us
    pallas_call x1, Pallas kernels, attend(): pl.pallas_call(attend_kernel, out_shape=(sds((rows, WIDE), bf16), sds((ro...  48.2 us
    pallas_call x1, Pallas kernels, attend_back(): pl.pallas_call(attend_back_kernel, out_shape=(sds((rows, WIDE), bf16), sd...  45.8 us
    unnamed x52, local copies, waits for them, and re-layouts  40.1 us
    pallas_call x1, Pallas kernels, out_back(): pl.pallas_call(out_back_kernel, out_shape=(sds((rows, WIDE), bf16), sds((...  23.2 us
  transfers between devices with their start and end apart: 19, of which 11 were waited for; matrix products, arithmetic and copies ran while one was open for 9% of the time, Pallas kernels for 22%

profile of v1, /device:TPU:0, one launch (start us, length us, event | category | flops | bytes accessed | tf_op | source)
XLA Modules:
  0.0 663.1 jit_solution(6600034737242430509)
XLA Ops:
  7.3 1.9 pad_maximum_fusion.1
  9.2 2.3 pad_maximum_fusion
  13.5 3.8 prep.1
  17.3 1.5 slice_reduce_fusion.1
  18.7 56.7 %all-gather.3.cloned.1.call-done = bf16[32,384,192]{2,1,0:T(8,128)(2,1)} async-done(((bf16[32,24,192]{2,1,0:T(8,128)(2,1)}), bf16[32,384,192]{2,1,0:T(8,128)(2,1)}) %all-gather.3.cloned.1.call-update) | async-done | bytes 4718608 | tf_op jit(solution)/shard_map/all_gather | solution.py:688
  75.4 1.0 slice_bitcast_fusion.3
  78.6 5.9 fusion.3
  84.5 48.2 %attend.1 = (bf16[4864,256]{1,0:T(8,128)(2,1)}, bf16[4864,256]{1,0:T(8,128)(2,1)}, f32[4864,128]{1,0:T(8,128)}, bf16[1024,256]{1,0:T(8,128)(2,1)}, bf16[1024,256...) custom-call(s32[2,16]{1,0:T(2,128)} %get-tuple-element.117.meta, bf16[1024,384]{1,0:T(8,128)(2,1)} %get-tuple-element.47.x_ref, ...), custom_call_target="tpu_custom_call" | custom-call | flops 30000001024 | bytes 20000000 | tf_op jit(solution)/shard_map/attend/pallas_call | solution.py:183
  132.7 15.6 %out_project.1.mine_ref = bf16[1024,384]{1,0:T(8,128)(2,1)} custom-call(s32[2,16]{1,0:T(2,128)} %get-tuple-element.117.meta, bf16[4864,256]{1,0:T(8,128)(2,1)} %get-tuple-element.49.o_ref, s32[16,1024]{1,0:T(8,128)} %get-tuple-element.48.cm_ref, f32[16,1024]{1,0:T(8,128)} %get-tuple-element.50.gate_ref, bf16[15,384,192]{2,1,0:T(8,128)(2,1)} %get-tuple-element.118.wo_ref), custom_call_target="tpu_custom_call" | custom-call | flops 8000000000 | bytes 8000000 | tf_op jit(solution)/shard_map/out_project/pallas_call | solution.py:222
  148.4 1.6 collective-permute-start
  151.9 1.2 bitcast_multiply_fusion.grad_ref.masked_ref
  153.0 15.1 %collective-permute-done.other_ref = bf16[1024,384]{1,0:T(8,128)(2,1)S(1)} collective-permute-done((bf16[1024,384]{1,0:T(8,128)(2,1)}, bf16[1024,384]{1,0:T(8,128)(2,1)S(1)}, u32[]{:S(2)}, u32[]{:S(2)}) %collective-permute-start) | collective-permute-done | bytes 786464 | tf_op jit(solution)/shard_map/ppermute | solution.py:648
  168.2 0.9 copy-done.16
  169.1 4.7 middle.1
  173.8 58.2 %feed.1 = (bf16[2,15,384,768]{3,2,1,0:T(8,128)(2,1)}, bf16[2,1024,384]{2,1,0:T(8,128)(2,1)}, f32[16,1024]{1,0:T(8,128)}) custom-call(s32[2,16]{1,0:T(2,128)} %get-tuple-element.116.meta, bf16[1024,768]{1,0:T(8,128)(2,1)} %get-tuple-element.53.x_ref, s32[16,1024]{1,0:T(8,128)} %get-tuple-element.51.cm_ref, f32[16,1024]{1,0:T(8,128)} %get-tuple-element.54.gate_ref, ...), custom_call_target="tpu_custom_call" | custom-call | flops 38000001024 | bytes 40000000 | tf_op jit(solution)/shard_map/feed/pallas_call | solution.py:329
  232.0 2.4 slice_bitcast_fusion.1
  234.5 1.6 collective-permute-start.2
  236.5 18.3 %collective-permute-done.3.ggo_ref = f32[16,1024]{1,0:T(8,128)S(1)} collective-permute-done((f32[16,1024]{1,0:T(8,128)S(1)}, f32[16,1024]{1,0:T(8,128)S(1)}, u32[]{:S(2)}, u32[]{:S(2)}) %collective-permute-start.3) | collective-permute-done | bytes 65568 | tf_op jit(solution)/shard_map/ppermute | solution.py:648
  255.7 6.2 second_back.1
  261.8 23.2 %out_back.1 = (bf16[4864,256]{1,0:T(8,128)(2,1)}, f32[4864,128]{1,0:T(8,128)}, f32[16,1024]{1,0:T(8,128)}, bf16[15,384,192]{2,1,0:T(8,128)(2,1)}) custom-call(s32[2,16]{1,0:T(2,128)} %get-tuple-element.117.meta, bf16[1024,384]{1,0:T(8,128)(2,1)} %get-tuple-element.58.mg_ref, s32[16,1024]{1,0:T(8,128)} %get-tuple-element.48.cm_ref, ...), custom_call_target="tpu_custom_call" | custom-call | flops 10000000000 | bytes 20000000 | tf_op jit(solution)/shard_map/out_back/pallas_call | solution.py:446
  285.1 45.8 %attend_back.1 = (bf16[4864,256]{1,0:T(8,128)(2,1)}, bf16[192,1024]{1,0:T(8,128)(2,1)}, bf16[192,1024]{1,0:T(8,128)(2,1)}) custom-call(s32[2,16]{1,0:T(2,128)} %get-tuple-element.117.meta, bf16[4864,256]{1,0:T(8,128)(2,1)} %get-tuple-element.56.q_ref, bf16[4864,256]{1,0:T(8,128)(2,1)} %get-tuple-element.59.do_ref, f32[4864,128]{1,0:T(8,128)} %get-tuple-element.60.lse_ref, ...), custom_call_target="tpu_custom_call" | custom-call | flops 60000002048 | bytes 20000000 | tf_op jit(solution)/shard_map/attend_back/pallas_call | solution.py:519
  330.9 20.6 %in_back.1 = (bf16[17,384,192]{2,1,0:T(8,128)(2,1)}, bf16[1024,384]{1,0:T(8,128)(2,1)}) custom-call(s32[2,16]{1,0:T(2,128)} %get-tuple-element.117.meta, bf16[4864,256]{1,0:T(8,128)(2,1)} %get-tuple-element.64.dq_ref, bf16[192,1024]{1,0:T(8,128)(2,1)} %get-tuple-element.65.dk_ref, bf16[192,1024]{1,0:T(8,128)(2,1)} %get-tuple-element.66.dv_ref, ...), custom_call_target="tpu_custom_call" | custom-call | flops 10000000000 | bytes 20000000 | tf_op jit(solution)/shard_map/in_back/pallas_call | solution.py:576
  351.5 6.2 copy.65
  357.6 7.5 %reshape.48 = bf16[384,3264]{1,0:T(8,128)(2,1)} reshape(bf16[384,17,192]{2,1,0:T(8,128)(2,1)} %bitcast.76) | data formatting | bytes 5013504
  365.2 16.1 %copy.56 = bf16[48,8,30,768]{3,1,2,0:T(8,128)(2,1)} copy(bf16[48,8,30,768]{3,1,0,2:T(8,128)(2,1)} %bitcast.77) | data formatting | bytes 35389440
  381.4 1.1 copy-done.13
  382.5 1.7 collective-permute-start.4
  384.5 1.7 collective-permute-start.1
  386.2 18.1 %collective-permute-done.5.ggo_ref = f32[16,1024]{1,0:T(8,128)S(1)} collective-permute-done((f32[16,1024]{1,0:T(8,128)S(1)}, f32[16,1024]{1,0:T(8,128)S(1)}, u32[]{:S(2)}, u32[]{:S(2)}) %collective-permute-start.5) | collective-permute-done | bytes 65568 | tf_op jit(solution)/shard_map/ppermute | solution.py:648
  405.0 3.0 route_back.1
  408.8 1.2 collective-permute-done.10
  410.1 0.9 collective-permute-start.11
  411.0 4.0 collective-permute-done.11
  415.0 1.7 collective-permute-start.12
  417.6 5.6 first_back.1
  423.2 1.4 collective-permute-done.6
  427.1 1.8 collective-permute-done.7
  429.5 1.1 maximum_select_fusion.1
  430.5 2.0 collective-permute-start.13
  432.6 1.0 collective-permute-start.9
  433.5 2.3 fusion
  435.9 15.4 %collective-permute-done.9 = f32[1,384]{1,0:T(1,128)S(1)} collective-permute-done((f32[1,384]{1,0:T(1,128)S(1)}, f32[1,384]{1,0:T(1,128)S(1)}, u32[]{:S(2)}, u32[]{:S(2)}) %collective-permute-start.9) | collective-permute-done | bytes 1568 | tf_op jit(solution)/shard_map/ppermute | solution.py:662
  455.4 1.7 convert_bitcast_fusion
  457.1 5.1 reduce-scatter.8.cloned.1.call-done
  462.2 1.1 reshape.49
  464.8 187.3 %reduce-scatter.10.cloned.1.call-done = bf16[24,23040]{1,0:T(8,128)(2,1)} async-done(((bf16[384,23040]{1,0:T(8,128)(2,1)}), bf16[24,23040]{1,0:T(8,128)(2,1)}) %reduce-scatter.10.cloned.1.call-update) | async-done | bytes 1105936
  652.1 1.9 reshape.53
  654.7 1.5 slice_bitcast_fusion
  (96 shorter events, 18.3 us)
Async XLA Ops:
  7.2 5.7 copy-start
  7.2 68.2 %all-gather.3.cloned.1.call-start = ((), (), s32[]{:S(2)}) async-start(), calls=%async_computation.2 | async-start | bytes 6684672 | tf_op jit(solution)/shard_map/all_gather | solution.py:688
  7.2 4.4 copy-start.10
  9.2 164.6 %all-gather.5.cloned.1.call-start = ((), (), s32[]{:S(2)}) async-start(), calls=%async_computation.3 | async-start | bytes 18800640 | tf_op jit(solution)/shard_map/all_gather | solution.py:689
  11.6 443.8 %all-reduce.7.cloned.1.call-start = ((), (), s32[]{:S(2)}) async-start(), calls=%async_computation.6 | async-start | bytes 5898240
  76.5 0.7 copy-start.6
  76.5 8.0 %copy-start.5 = (bf16[384,192]{1,0:T(8,128)(2,1)}, bf16[384,192]{1,0:T(8,128)(2,1)S(1)}, u32[]{:S(2)}) copy-start(bf16[384,192]{1,0:T(8,128)(2,1)S(1)} %get-tuple-element.120.wv_ref) | copy-start | bytes 442372
  132.7 17.2 %copy-start.11 = (f32[384]{0:T(512)S(1)}, f32[384]{0:T(512)}, u32[]{:S(2)}) copy-start(f32[384]{0:T(512)} %param.28) | copy-start | bytes 4612
  132.7 19.1 %copy-start.9 = (s32[1,1024]{1,0:T(1,128)S(1)}, s32[1,1024]{1,0:T(1,128)}, u32[]{:S(2)}) copy-start(s32[1,1024]{1,0:T(1,128)} %param.21) | copy-start | bytes 12292
  132.7 19.2 %copy-start.4 = (bf16[1,1024,384]{2,1,0:T(8,128)(2,1)S(1)}, bf16[1,1024,384]{2,1,0:T(8,128)(2,1)}, u32[]{:S(2)}) copy-start(bf16[1,1024,384]{2,1,0:T(8,128)(2,1)} %param.17) | copy-start | bytes 2359300
  148.4 19.8 %collective-permute-start = (bf16[1024,384]{1,0:T(8,128)(2,1)}, bf16[1024,384]{1,0:T(8,128)(2,1)S(1)}, u32[]{:S(2)}, u32[]{:S(2)}) collective-permute-start(bf16[1024,384]{1,0:T(8,128)(2,1)} %out_project.1.mine_ref), channel_id=1, source_target_pairs={{0,1},{1,0},{2,3},{3,2},{4,5},{5,4},{6,7},{7,6},{8,9},{9,8},{10,11... | collective-permute-start | bytes 2359304 | tf_op jit(solution)/shard_map/ppermute | solution.py:648
  168.2 0.9 copy-start.16
  232.0 4.0 copy-start.18
  234.5 20.3 %copy-start.7 = (bf16[1024,384]{1,0:T(8,128)(2,1)}, bf16[1024,384]{1,0:T(8,128)(2,1)S(1)}, u32[]{:S(2)}) copy-start(bf16[1024,384]{1,0:T(8,128)(2,1)S(1)} %get-tuple-element.124.mine_ref) | copy-start | bytes 2359300
  234.5 20.3 %collective-permute-start.2 = (bf16[1024,384]{1,0:T(8,128)(2,1)S(1)}, bf16[1024,384]{1,0:T(8,128)(2,1)S(1)}, u32[]{:S(2)}, u32[]{:S(2)}) collective-permute-start(bf16[1024,384]{1,0:T(8,128)(2,1)S(1)} %get-tuple-element.124.mine_ref), channel_id=1, source_target_pairs={{0,1},{1,0},{2,3},{3,2},{4,5},{5,4},{6,7},{7,6},{8,9},{9,8},{10,11... | collective-permute-start | bytes 2359304 | tf_op jit(solution)/shard_map/ppermute | solution.py:648
  236.0 18.7 %collective-permute-start.3 = (f32[16,1024]{1,0:T(8,128)S(1)}, f32[16,1024]{1,0:T(8,128)S(1)}, u32[]{:S(2)}, u32[]{:S(2)}) collective-permute-start(f32[16,1024]{1,0:T(8,128)S(1)} %copy-done.18), channel_id=1, source_target_pairs={{0,1},{1,0},{2,3},{3,2},{4,5},{5,4},{6,7},{7,6},{8,9},{9,8},{10,11... | collective-permute-start | bytes 196616 | tf_op jit(solution)/shard_map/ppermute | solution.py:648
  254.7 0.6 copy-start.19
  254.8 0.9 copy-start.15
  285.1 177.1 %reduce-scatter.8.cloned.1.call-start = ((), (), s32[]{:S(2)}) async-start(), calls=%async_computation.4 | async-start | bytes 2715648
  365.2 287.0 %reduce-scatter.10.cloned.1.call-start = ((), (), s32[]{:S(2)}) async-start(), calls=%async_computation.5 | async-start | bytes 18800640
  381.3 1.1 copy-start.13
  381.3 2.8 copy-start.17
  382.5 34.3 %collective-permute-start.4 = (bf16[1024,384]{1,0:T(8,128)(2,1)S(1)}, bf16[1024,384]{1,0:T(8,128)(2,1)S(1)}, u32[]{:S(2)}, u32[]{:S(2)}) collective-permute-start(bf16[1024,384]{1,0:T(8,128)(2,1)S(1)} %copy-done.13), channel_id=1, source_target_pairs={{0,1},{1,0},{2,3},{3,2},{4,5},{5,4},{6,7},{7,6},{8,9},{9,8},{10,11... | collective-permute-start | bytes 2359304 | tf_op jit(solution)/shard_map/ppermute | solution.py:648
  384.1 20.2 %collective-permute-start.5 = (f32[16,1024]{1,0:T(8,128)S(1)}, f32[16,1024]{1,0:T(8,128)S(1)}, u32[]{:S(2)}, u32[]{:S(2)}) collective-permute-start(f32[16,1024]{1,0:T(8,128)S(1)} %copy-done.17), channel_id=1, source_target_pairs={{0,1},{1,0},{2,3},{3,2},{4,5},{5,4},{6,7},{7,6},{8,9},{9,8},{10,11... | collective-permute-start | bytes 196616 | tf_op jit(solution)/shard_map/ppermute | solution.py:648
  384.5 23.5 %copy-start.8 = (f32[16,384]{1,0:T(8,128)S(1)}, f32[16,384]{1,0:T(8,128)}, u32[]{:S(2)}) copy-start(f32[16,384]{1,0:T(8,128)} %get-tuple-element.77) | copy-start | bytes 73732
  384.5 23.5 %copy-start.12 = (f32[1,384]{1,0:T(1,128)S(1)}, f32[1,384]{1,0:T(1,128)}, u32[]{:S(2)}) copy-start(f32[1,384]{1,0:T(1,128)} %get-tuple-element.78) | copy-start | bytes 4612
  384.5 49.0 %collective-permute-start.1 = (bf16[1024,384]{1,0:T(8,128)(2,1)}, bf16[1024,384]{1,0:T(8,128)(2,1)}, u32[]{:S(2)}, u32[]{:S(2)}) collective-permute-start(bf16[1024,384]{1,0:T(8,128)(2,1)} %get-tuple-element.125), channel_id=1, source_target_pairs={{0,1},{1,0},{2,3},{3,2},{4,5},{5,4},{6,7},{7,6},{8,9},{9,8},{10,11... | collective-permute-start | bytes 2359304 | tf_op jit(solution)/shard_map/ppermute | solution.py:648
  404.3 0.6 copy-start.20
  408.8 1.3 collective-permute-start.10
  410.1 4.9 collective-permute-start.11
  415.0 14.4 %collective-permute-start.12 = (f32[4,32,384]{2,1,0:T(8,128)S(1)}, f32[4,32,384]{2,1,0:T(8,128)}, u32[]{:S(2)}, u32[]{:S(2)}) collective-permute-start(f32[4,32,384]{2,1,0:T(8,128)S(1)} %maximum_select_fusion.2), channel_id=1, source_target_pairs={{0,8},{2,10},{4,12},{6,14},{8,0},{10,2},{12,4},{14,6},{16,24},{18,... | collective-permute-start | bytes 589832 | tf_op jit(solution)/shard_map/ppermute | solution.py:670
  416.7 0.9 copy-start.14
  417.6 8.2 %copy-start.21 = (u32[32]{0:T(128)S(1)}, u32[32]{0:T(128)}, u32[]{:S(2)}) copy-start(u32[32]{0:T(128)} %constant.106) | copy-start | bytes 388
  417.6 15.9 %copy-start.2 = (bf16[2,1024,384]{2,1,0:T(8,128)(2,1)S(1)}, bf16[2,1024,384]{2,1,0:T(8,128)(2,1)}, u32[]{:S(2)}) copy-start(bf16[2,1024,384]{2,1,0:T(8,128)(2,1)} %get-tuple-element.55) | copy-start | bytes 4718596
  417.6 15.9 %copy-start.3 = (f32[1024,384]{1,0:T(8,128)S(1)}, f32[1024,384]{1,0:T(8,128)}, u32[]{:S(2)}) copy-start(f32[1024,384]{1,0:T(8,128)} %get-tuple-element.52.mid_ref) | copy-start | bytes 4718596
  423.2 1.4 collective-permute-start.6
  425.2 3.6 collective-permute-start.7
  428.8 3.7 collective-permute-start.8
  430.5 21.4 %collective-permute-start.13 = (f32[8,32,384]{2,1,0:T(8,128)S(1)}, f32[8,32,384]{2,1,0:T(8,128)S(1)}, u32[]{:S(2)}, u32[]{:S(2)}) collective-permute-start(f32[8,32,384]{2,1,0:T(8,128)S(1)} %maximum_select_fusion.1), channel_id=1, source_target_pairs={{0,16},{2,18},{4,20},{6,22},{8,24},{10,26},{12,28},{14,30},{16,0},... | collective-permute-start | bytes 1179656 | tf_op jit(solution)/shard_map/ppermute | solution.py:670
  432.6 18.7 %collective-permute-start.9 = (f32[1,384]{1,0:T(1,128)S(1)}, f32[1,384]{1,0:T(1,128)S(1)}, u32[]{:S(2)}, u32[]{:S(2)}) collective-permute-start(f32[1,384]{1,0:T(1,128)S(1)} %add.59), channel_id=1, source_target_pairs={{0,16},{2,18},{4,20},{6,22},{8,24},{10,26},{12,28},{14,30},{16,0},... | collective-permute-start | bytes 4616 | tf_op jit(solution)/shard_map/ppermute | solution.py:662
  654.0 2.2 copy-start.1
Sparse Core Ops, SparseCore 0:
  10.9 64.4 all-gather.2
  77.6 91.8 all-gather.4
  285.2 101.4 all-reduce.6
  390.4 71.7 reduce-scatter.7
  466.8 185.2 reduce-scatter.9
